TPU v7x, 32 devices: a whole 2x2x4 slice. The times are simulated.
32 devices in a mesh: wide: 8 (over z, y), narrow: 4 (over x, core).
Axes of the slice: x: 2, y: 2, z: 4, core: 2. Of those that a mesh axis runs over, the one named last changes fastest.
Arguments:
- features: bfloat16 [8192, 2048], P(('wide', 'narrow')), may hold values from -6 to 6
- projection: bfloat16 [2048, 32], replicated, may hold values from -0.125 to 0.125
- targets: float32 [8192], P(('wide', 'narrow')), may hold values from -9 to 9
Outputs:
- solution: float32 [8192], P(('wide', 'narrow'))
- residual: float32 [8192], P(('wide', 'narrow'))
All inputs are finite; a program needn't handle non-finite values.
Results may differ from a plain program's by a relative error of at most 0.0003.
Values sent between devices are 32-bit elements; how exact they have to be, the bound alone decides.
No kernel may reach another device: no remote copies, remote signals or barrier semaphores. Data moves between devices by JAX's collectives and lax.ppermute only.
A program may use at most 64 MiB of HBM per device.

v0:
```python
import functools
import math

import jax
import jax.numpy as jnp
import numpy as np
from jax import lax
from jax.experimental import pallas as pl
from jax.experimental.pallas import tpu as pltpu
from jax.sharding import PartitionSpec as P

noise_var = 0.5
LANES = 128
TOGETHER = 2
EARLY = 10**9
DIRECT = 8
KEEP_BYTES = 8 * 2**20
VMEM_BYTES = 32 * 2**20
WHOLE_VMEM_BYTES = (53 * 1024 + 835) * 2**10
ALL = "all"
HIGH, LOW, Y, X, CORE = range(5)
highest = lax.Precision.HIGHEST
f32 = jnp.float32
bf16 = jnp.bfloat16


def split3(values):
    high = values.astype(bf16)
    rest = values - high.astype(f32)
    mid = rest.astype(bf16)
    low = (rest - mid.astype(f32)).astype(bf16)
    return high, mid, low


def exponent_rows(first, second):
    width = (first if not isinstance(first, float) else second).shape[1]
    row = lax.broadcasted_iota(jnp.int32, (16, width), 0)
    out = jnp.zeros((16, width), f32)
    for base, value in ((0, first), (3, second)):
        parts = (1.0, 1.0, 1.0) if isinstance(value, float) else [p.astype(f32) for p in split3(value)]
        for k, part in enumerate(parts):
            out = jnp.where(row == base + k, part, out)
    return out.astype(bf16)


def right_operand(latent, scale):
    square = jnp.sum(latent * latent, axis=0, keepdims=True) * scale
    h, m, l = split3(latent)
    return jnp.concatenate([h, m, l, h, m, h, exponent_rows(square, 1.0)], axis=0)


def left_operand(latent, scale):
    square = jnp.sum(latent * latent, axis=0, keepdims=True) * scale
    h, m, l = split3(latent * (-2.0 * scale))
    stacked = jnp.concatenate([h, h, h, m, m, l, exponent_rows(1.0, square)], axis=0)
    return stacked.T


def axis_sizes(wide, narrow):
    return 2, wide // 4, 2, narrow // 2, 2


def place(wide, narrow):
    rest, out = lax.axis_index(ALL), []
    for size in reversed(axis_sizes(wide, narrow)):
        out.append(rest % size)
        rest = rest // size
    return tuple(reversed(out))


def device_at(high, low, y, x, core, wide, narrow):
    return (((high * (wide // 4) + low) * 2 + y) * (narrow // 2) + x) * 2 + core


def slot(device, wide, narrow):
    return wide * narrow - 1 - device


def part_base(part, parts, wide, narrow):
    return 0 if parts == 1 else jnp.bitwise_xor(place(wide, narrow)[X], part) * 2


def row_sources(blocks, flips, wide, narrow):
    spots = [(b, i) for b in blocks for i in range(b.shape[0])]
    if flips is None:
        return [(b, i, i) for b, i in spots]
    high = place(wide, narrow)[HIGH]
    return [(b, i, jnp.bitwise_xor(high, flip)) for (b, i), flip in zip(spots, flips)]


def column_sources(blocks, flips, wide, narrow):
    spots = [(b, i) for b in blocks for i in range(b.shape[0])]
    if flips is None:
        return [(b, i, i) for b, i in spots]
    _, low, y, _, _ = place(wide, narrow)
    return [(b, i, jnp.bitwise_xor(low * 2 + y, flip)) for (b, i), flip in zip(spots, flips)]


def total_sum(values):
    return jnp.sum(jnp.sum(values, axis=0, keepdims=True), axis=1, keepdims=True)


def lane_sums(values):
    parts = jnp.concatenate(split3(values), axis=1)
    ones = jnp.ones((16, parts.shape[1]), bf16)
    return lax.dot_general(ones, parts, (((1,), (1,)), ((), ())),
                           preferred_element_type=f32)[0:1, :]


def make_rows(left, right, kept, read_vector, sums, add):
    groups, rows, _ = left.shape
    columns = right.shape[0]
    halves = rows // LANES

    def one_group(g, _):
        left_group = left[g]

        def some_columns(step, acc):
            first = step * TOGETHER
            both = jnp.concatenate([right[first + k] for k in range(TOGETHER)], axis=1)
            exponent = jnp.dot(left_group, both, preferred_element_type=f32)
            tile = jnp.exp2(exponent)
            for k in range(TOGETHER):
                if kept is not None:
                    kept[g, first + k] = tile[:, k * rows:(k + 1) * rows]
                for half in range(halves):
                    start = k * rows + half * LANES
                    acc = acc + tile[:, start:start + LANES] * read_vector(first + k, half)
            return acc

        start_sum = sums[g] if add else jnp.zeros((rows, LANES), f32)
        sums[g] = lax.fori_loop(0, columns // TOGETHER, some_columns, start_sum,
                                unroll=4 // TOGETHER)
        return 0

    lax.fori_loop(0, groups, one_group, 0, unroll=groups <= 2)


def use_rows(kept, read_vector, sums, add):
    groups, columns, rows, _ = kept.shape
    halves = rows // LANES

    def one_group(g, _):
        def one_column(c, acc):
            for half in range(halves):
                acc = acc + kept[g, c, :, half * LANES:(half + 1) * LANES] * read_vector(c, half)
            return acc

        start_sum = sums[g] if add else jnp.zeros((rows, LANES), f32)
        sums[g] = lax.fori_loop(0, columns, one_column, start_sum, unroll=4)
        return 0

    lax.fori_loop(0, groups, one_group, 0, unroll=groups <= 2)


def write_rows(sums, out, bases):
    groups, rows, _ = sums.shape
    halves = rows // LANES
    total = lane_sums(sums[...].reshape(groups * rows, LANES))
    for g in range(groups):
        base = bases[g * len(bases) // groups]
        for half in range(halves):
            line = (base + g % (groups // len(bases))) * halves + half
            start = (g * halves + half) * LANES
            out[pl.ds(line, 1), :] = total[:, start:start + LANES]


def project_kernel(features, projection_t, targets, latent, out, feature_buf, projection_buf, target_buf, sems):
    proj = projection_t.shape[0]
    chunks, height, _ = feature_buf.shape
    copies = [
        pltpu.make_async_copy(features.at[pl.ds(i * height, height)], feature_buf.at[i], sems.at[i])
        for i in range(chunks)]
    copies.insert(1, pltpu.make_async_copy(projection_t, projection_buf, sems.at[chunks]))
    copies.append(pltpu.make_async_copy(targets, target_buf, sems.at[chunks + 1]))
    for copy in copies:
        copy.start()
    copies.pop(1).wait()
    for i in range(chunks):
        copies[i].wait()
        some = lax.dot_general(
            projection_buf[...], feature_buf[i], (((1,), (1,)), ((), ())), preferred_element_type=f32)
        latent[0, i * proj:(i + 1) * proj, :] = some
        out[0, i * proj:(i + 1) * proj, :] = some
    copies[-1].wait()
    line = lax.broadcasted_iota(jnp.int32, (8, LANES), 0)
    tail = jnp.zeros((8, LANES), f32)
    for i in range(chunks):
        tail = jnp.where(line == i, target_buf[:, i * LANES:(i + 1) * LANES], tail)
    out[0, chunks * proj:, :] = tail


def block_latent(block, i, proj, halves):
    return jnp.concatenate([block[i, half * proj:(half + 1) * proj, :] for half in range(halves)], axis=1)


def prepare_rows(blocks, flips, left, proj, scale, wide, narrow):
    for block, i, source in row_sources(blocks, flips, wide, narrow):
        left[source] = left_operand(block_latent(block, i, proj, left.shape[1] // LANES), scale)


def vector_reader(vector, halves):
    return lambda c, half: vector[pl.ds(c * halves + half, 1), :]


def side_kernel(proj, scale, wide, narrow, keep, flips, row_count, column_count, *refs):
    rows_in, columns_in = refs[:row_count], refs[row_count:row_count + column_count]
    refs = refs[row_count + column_count:]
    fresh = rows_in[0].dtype == f32
    left, refs = (refs[0], refs[1:]) if fresh else (rows_in[0], refs)
    right, vector, partial, sums = refs[0], refs[1], refs[2], refs[-1]
    kept = refs[3] if keep else None
    halves = left.shape[1] // LANES
    if fresh:
        prepare_rows(rows_in, flips[0], left, proj, scale, wide, narrow)
    for block, i, source in column_sources(columns_in, flips[1], wide, narrow):
        right[source] = right_operand(block_latent(block, i, proj, halves), scale)
        for half in range(halves):
            line = halves * proj + half
            vector[pl.ds(source * halves + half, 1), :] = block[i, line:line + 1, :]
    make_rows(left, right, kept, vector_reader(vector, halves), sums, False)
    write_rows(sums, partial, [0])


def rest_kernel(proj, scale, wide, narrow, keep, flips, *refs):
    rows_in, columns, refs = refs[:1], refs[1:5], refs[5:]
    if keep:
        partial, *kept, sums, left = refs
    else:
        left, partial, sums = refs
        kept = (None, None)
    halves = left.shape[1] // LANES
    prepare_rows(rows_in, flips[0], left, proj, scale, wide, narrow)
    for side in range(2):
        right, vector = columns[2 * side:2 * side + 2]
        make_rows(left, right, kept[side], vector_reader(vector, halves), sums, side > 0)
    write_rows(sums, partial, [0])


def message_kernel(parts, wide, narrow, halves, *refs):
    partials, vector, out, held = refs[:parts + 1], refs[parts + 1], refs[-2], refs[-1]
    lines_of = [partials[0][...] + partials[1][...]] + [partial[...] for partial in partials[2:]]
    for part, lines in enumerate(lines_of):
        base = part_base(part, parts, wide, narrow) * halves
        for line in range(lines.shape[0]):
            held[pl.ds(base + line, 1), :] = lines[line:line + 1, :]
    _, low, y, _, _ = place(wide, narrow)
    mine = (low * 2 + y) * halves
    pieces = [held[line:line + 1, :] for line in range(held.shape[0])]
    pieces += [vector[pl.ds(mine + half, 1), :] for half in range(halves)]
    block = jnp.concatenate(pieces, axis=1)

    def copy(i, _):
        out[i] = block
        return 0

    lax.fori_loop(0, out.shape[0], copy, 0, unroll=8)


def second_kernel(wide, narrow, keep, parts, *refs):
    arrived, out, step_scalars, direction, images, targets, partial, sums = refs[:1] + refs[-7:]
    lines = partial.shape[0]
    halves = lines // narrow
    across = narrow // 2
    group = [(high, x) for x in range(narrow // 2) for high in range(2)]

    def unpack(low, _):
        for y, core in ((0, 0), (0, 1), (1, 0), (1, 1)):
            members = [device_at(high, low, y, x, core, wide, narrow) for high, x in group]
            slots = [slot(member, wide, narrow) for member in members]
            total = arrived[slots[0], :, 0:lines * LANES]
            for spot in slots[1:]:
                total = total + arrived[spot, :, 0:lines * LANES]
            for r, member in enumerate(members):
                for half in range(halves):
                    start = arrived[slots[r], :, (lines + half) * LANES:(lines + half + 1) * LANES]
                    line = r * halves + half
                    spot = pl.ds(member * halves + half, 1)
                    targets[spot, :] = start
                    images[spot, :] = total[:, line * LANES:(line + 1) * LANES] + noise_var * start
        return 0

    lax.fori_loop(0, wide // 4, unpack, 0, unroll=2)
    start, first = targets[...], images[...]
    norm = total_sum(start * start)
    alpha = norm / total_sum(start * first)
    residual = start - alpha * first
    norm_next = total_sum(residual * residual)
    beta = norm_next / norm
    whole = residual + beta * start
    direction[...] = whole
    high, low, y, x, core = place(wide, narrow)

    def side_reader(side):
        def read_vector(c, half):
            source = device_at(high, c // 2, c % 2, x, jnp.bitwise_xor(core, side), wide, narrow)
            return direction[pl.ds(source * halves + half, 1), :]
        return read_vector

    groups = narrow // parts
    for part in range(parts):
        part_sums = sums.at[part * groups:(part + 1) * groups]
        for side in range(2):
            if keep:
                use_rows(refs[1 + 2 * part + side], side_reader(side), part_sums, side > 0)
            else:
                make_rows(refs[3 + part], refs[1 + side], None, side_reader(side), part_sums, side > 0)
    write_rows(sums, partial, [part_base(part, parts, wide, narrow) for part in range(parts)])
    share = jnp.zeros((1, LANES), f32)
    for r, (row_high, row_x) in enumerate(group):
        for half in range(halves):
            spot = pl.ds(device_at(row_high, low, y, row_x, core, wide, narrow) * halves + half, 1)
            line = r * halves + half
            share = share + direction[spot, :] * partial[line:line + 1, :]
    blocks = [
        jnp.concatenate([partial[r * halves + half:r * halves + half + 1, :]
                         for half in range(halves)] + [share], axis=1)
        for r in range(narrow)]

    def copy(to_low, _):
        for r, (to_high, to_x) in enumerate(group):
            for to_y, to_core in ((0, 0), (0, 1), (1, 0), (1, 1)):
                to = device_at(to_high, to_low, to_y, to_x, to_core, wide, narrow)
                out[slot(to, wide, narrow)] = blocks[r]
        return 0

    lax.fori_loop(0, wide // 4, copy, 0, unroll=2)
    lane = lax.broadcasted_iota(jnp.int32, (1, LANES), 1)
    noise = noise_var * total_sum(whole * whole)
    step_scalars[0:1, :] = jnp.where(lane == 0, alpha, jnp.where(
        lane == 1, norm_next, jnp.where(lane == 2, beta, noise)))
    for half in range(halves):
        spot = pl.ds(device_at(high, low, y, x, core, wide, narrow) * halves + half, 1)
        step_scalars[1 + half:2 + half, :] = images[spot, :]
        step_scalars[1 + halves + half:2 + halves + half, :] = targets[spot, :]


def last_kernel(wide, narrow, arrived, step_scalars, solution_out, residual_out, answer, sems):
    alpha = step_scalars[0:1, 0:1]
    norm = step_scalars[0:1, 1:2]
    beta = step_scalars[0:1, 2:3]
    noise = step_scalars[0:1, 3:4]
    halves = answer.shape[1]

    def add(i, total):
        return total + arrived[i, :, halves * LANES:(halves + 1) * LANES]

    share = lax.fori_loop(0, arrived.shape[0], add, jnp.zeros((1, LANES), f32), unroll=32)
    alpha_next = norm / (total_sum(share) + noise)
    _, low, y, _, core = place(wide, narrow)
    product = jnp.zeros((1, (halves + 1) * LANES), f32)
    for high in range(2):
        for x in range(narrow // 2):
            member = device_at(high, low, y, x, core, wide, narrow)
            product = product + arrived[slot(member, wide, narrow)]
    for half in range(halves):
        begin = step_scalars[1 + halves + half:2 + halves + half, :]
        residual = begin - alpha * step_scalars[1 + half:2 + half, :]
        direction = residual + beta * begin
        image = product[:, half * LANES:(half + 1) * LANES] + noise_var * direction
        answer[0, half:half + 1, :] = alpha * begin + alpha_next * direction
        answer[1, half:half + 1, :] = residual - alpha_next * image
    copies = [pltpu.make_async_copy(answer.at[i], out, sems.at[i])
              for i, out in enumerate((solution_out, residual_out))]
    for copy in copies:
        copy.start()
    for copy in copies:
        copy.wait()


def call(kernel, out_shape, *args, scratch=(), vmem=VMEM_BYTES, **options):
    return pl.pallas_call(
        kernel,
        out_shape=out_shape,
        scratch_shapes=list(scratch),
        compiler_params=pltpu.CompilerParams(vmem_limit_bytes=vmem),
        **options,
    )(*args)


def to_all(blocks):
    group = list(range(blocks.shape[0] - 1, -1, -1))
    return lax.all_to_all(blocks, ALL, split_axis=0, concat_axis=0, axis_index_groups=[group], tiled=True)


def join_kernel(*refs):
    i = 0
    for block in refs[:-1]:
        for j in range(block.shape[0]):
            refs[-1][i] = block[j]
            i += 1


def join(*blocks, flops=0):
    total = sum(b.shape[0] for b in blocks)
    return call(join_kernel, jax.ShapeDtypeStruct((total, *blocks[0].shape[1:]), f32), *blocks,
                cost_estimate=pl.CostEstimate(flops=flops, bytes_accessed=0, transcendentals=0))


def first_round(latent, own, wide, narrow):
    lows, across = wide // 4, narrow // 2
    if lows & (lows - 1) or across != 2 or lows > DIRECT:
        every = lax.all_gather(own, ALL, axis=0, tiled=True)
        every = every.reshape(2, lows, 2, across, 2, *own.shape[1:])
        high, low, y, x, core = place(wide, narrow)
        rows = every
        for place_in, axis in ((low, 1), (y, 1), (core, 2)):
            rows = lax.dynamic_index_in_dim(rows, place_in, axis, keepdims=False)
        columns = lax.dynamic_index_in_dim(every, high, 0, keepdims=False)
        columns = lax.dynamic_index_in_dim(columns, x, 2, keepdims=False)
        rows = jnp.swapaxes(rows, 0, 1).reshape(narrow, *own.shape[1:])
        sides = [lax.dynamic_index_in_dim(columns, jnp.bitwise_xor(core, side), 2, keepdims=False)
                 for side in range(2)]
        sides = [[columns.reshape(wide // 2, *own.shape[1:])] for columns in sides]
        return [[rows]], sides, (None, None)

    sizes = axis_sizes(wide, narrow)

    def swap(value, **flips):
        pairs = []
        for i in range(wide * narrow):
            spot = list(np.unravel_index(i, sizes))
            for name, flip in flips.items():
                axis = dict(high=HIGH, low=LOW, y=Y, x=X, core=CORE)[name]
                spot[axis] = int(spot[axis]) ^ flip
            pairs.append((i, int(np.ravel_multi_index(spot, sizes))))
        return lax.ppermute(value, ALL, pairs)

    rows = join(latent, swap(latent, high=1), flops=EARLY)
    columns = [own] + [swap(own, low=flip // 2, y=flip % 2) for flip in range(1, 2 * lows)]
    sides = [columns, [swap(block, core=1) for block in columns]]
    parts = [[rows], [swap(rows, x=1)]]
    return parts, sides, ([0, 1], list(range(2 * lows)))


def on_device(wide, narrow, features, projection, targets):
    rows, proj = features.shape[0], projection.shape[1]
    halves = rows // LANES
    lines = narrow * halves
    devices = wide * narrow
    scale = -2.0 / proj * math.log2(math.e)
    depth = 6 * proj + 16
    keep = 4 * devices * rows * rows <= KEEP_BYTES

    def shape(*dims, dtype=f32):
        return jax.ShapeDtypeStruct(dims, dtype)

    def scratch(*dims, dtype=f32):
        return pltpu.VMEM(dims, dtype)

    feat = features.shape[1]
    latent, own = call(
        project_kernel, (shape(1, halves * proj, LANES), shape(1, halves * proj + 8, LANES)), features, projection.T, targets.reshape(1, rows),
        in_specs=[pl.BlockSpec(memory_space=pl.ANY)] * 3, vmem=WHOLE_VMEM_BYTES,
        scratch=[scratch(halves, LANES, feat, dtype=bf16), scratch(proj, feat, dtype=bf16),
                 scratch(1, rows), pltpu.SemaphoreType.DMA((halves + 2,))])
    row_parts, sides, flips = first_round(latent, own, wide, narrow)
    parts = len(row_parts)
    groups = narrow // parts
    left = shape(groups, rows, depth, dtype=bf16)
    right = shape(wide // 2, depth, rows, dtype=bf16)
    vector = shape(wide // 2 * halves, LANES)
    kept = (shape(groups, wide // 2, rows, rows),) if keep else ()
    group_lines = shape(groups * halves, LANES)
    sums = scratch(groups, rows, LANES)
    settings = (proj, scale, wide, narrow, keep, flips)

    def cost(columns):
        tiles = groups * columns * rows * rows
        return pl.CostEstimate(flops=2 * tiles * depth, bytes_accessed=4 * tiles, transcendentals=tiles)

    lefts, columns, blocks, partials = [], [], [], []
    for side, column_blocks in enumerate(sides):
        row_blocks = row_parts[0] if side == 0 else lefts
        made = call(
            functools.partial(side_kernel, *settings, len(row_blocks), len(column_blocks)),
            ((left,) if side == 0 else ()) + (right, vector, group_lines) + kept,
            *row_blocks, *column_blocks, scratch=[sums], cost_estimate=cost(wide // 2))
        if side == 0:
            lefts, made = [made[0]], made[1:]
        columns += made[:2]
        partials.append(made[2])
        blocks += made[3:]
    for row_blocks in row_parts[1:]:
        made = call(
            functools.partial(rest_kernel, *settings),
            (group_lines, *kept * 2) if keep else (left, group_lines), *row_blocks, *columns,
            scratch=[sums, scratch(*left.shape, dtype=bf16)] if keep else [sums],
            cost_estimate=cost(wide))
        if not keep:
            lefts.append(made[0])
        partials.append(made[0 if keep else 1])
        blocks += made[1:] if keep else []
    out = call(
        functools.partial(message_kernel, parts, wide, narrow, halves),
        shape(devices, 1, (lines + halves) * LANES), *partials, columns[1],
        scratch=[scratch(lines, LANES)])
    block = blocks if keep else [columns[0], columns[2], *lefts]
    sums = scratch(narrow, rows, LANES)
    out, step_scalars = call(
        functools.partial(second_kernel, wide, narrow, keep, parts),
        (shape(devices, 1, (halves + 1) * LANES), shape(1 + 2 * halves, LANES)),
        to_all(out), *block,
        scratch=[scratch(devices * halves, LANES)] * 3 + [scratch(lines, LANES), sums])
    answer, residual = call(
        functools.partial(last_kernel, wide, narrow), (shape(halves, LANES), shape(halves, LANES)),
        to_all(out), step_scalars,
        out_specs=(pl.BlockSpec(memory_space=pl.ANY),) * 2,
        scratch=[scratch(2, halves, LANES), pltpu.SemaphoreType.DMA((2,))])
    return answer.reshape(rows), residual.reshape(rows)


def solution(mesh):
    wide, narrow = mesh.shape["wide"], mesh.shape["narrow"]
    line = jax.sharding.Mesh(mesh.devices.reshape(wide * narrow), (ALL,))
    in_specs = (P(ALL, None), P(), P(ALL))
    return jax.shard_map(
        functools.partial(on_device, wide, narrow), mesh=line,
        in_specs=in_specs, out_specs=(P(ALL), P(ALL)), check_vma=False,
    )
```

profile of v0, /device:TPU:0, one launch (start us, length us, event | category | flops | bytes accessed | tf_op | source)
XLA Modules:
  0.0 40.7 jit_solution(18007017816577740495)
XLA Ops:
  0.6 0.7 %copy-done = f32[256]{0:T(256)S(1)} copy-done((f32[256]{0:T(256)S(1)}, f32[256]{0:T(256)}, u32[]{:S(2)}) %copy-start) | copy-done | bytes 1048
  1.3 1.9 %shard_map.50 = (f32[1,64,128]{2,1,0:T(8,128)S(1)}, f32[1,72,128]{2,1,0:T(8,128)S(1)}) custom-call(bf16[256,2048]{1,0:T(8,128)(2,1)} %features.1, bf16[32,2048]{1,0:T(8,128)(2,1)} %bitcast.5, f32[1,256]{1,0:T(1,128)S(1)} %bitcast.4), custom_call_target="tpu_custom_call" | custom-call | tf_op jit(solution)/shard_map/pallas_call | solution.py:372
  3.2 4.1 %collective-permute-start = (f32[1,64,128]{2,1,0:T(8,128)S(1)}, f32[1,64,128]{2,1,0:T(8,128)S(1)}, u32[]{:S(2)}, u32[]{:S(2)}) collective-permute-start(f32[1,64,128]{2,1,0:T(8,128)S(1)} %get-tuple-element.20.refs_0_), channel_id=1, source_target_pairs={{0,16},{1,17},{2,18},{3,19},{4,20},{5,21},{6,22},{7,23},{8,24},{9,... | collective-permute-start | bytes 98312 | tf_op jit(solution)/shard_map/ppermute | solution.py:427
  7.3 2.5 %collective-permute-start.3 = (f32[1,72,128]{2,1,0:T(8,128)S(1)}, f32[1,72,128]{2,1,0:T(8,128)S(1)}, u32[]{:S(2)}, u32[]{:S(2)}) collective-permute-start(f32[1,72,128]{2,1,0:T(8,128)S(1)} %get-tuple-element.21.refs_1_), channel_id=1, source_target_pairs={{0,12},{1,13},{2,14},{3,15},{4,8},{5,9},{6,10},{7,11},{8,4},{9,5},... | collective-permute-start | bytes 110600 | tf_op jit(solution)/shard_map/ppermute | solution.py:427
  9.8 0.4 %collective-permute-start.2 = (f32[1,72,128]{2,1,0:T(8,128)S(1)}, f32[1,72,128]{2,1,0:T(8,128)S(1)}, u32[]{:S(2)}, u32[]{:S(2)}) collective-permute-start(f32[1,72,128]{2,1,0:T(8,128)S(1)} %get-tuple-element.21.refs_1_), channel_id=1, source_target_pairs={{0,8},{1,9},{2,10},{3,11},{4,12},{5,13},{6,14},{7,15},{8,0},{9,1},... | collective-permute-start | bytes 110600 | tf_op jit(solution)/shard_map/ppermute | solution.py:427
  10.3 0.5 %collective-permute-start.1 = (f32[1,72,128]{2,1,0:T(8,128)S(1)}, f32[1,72,128]{2,1,0:T(8,128)S(1)}, u32[]{:S(2)}, u32[]{:S(2)}) collective-permute-start(f32[1,72,128]{2,1,0:T(8,128)S(1)} %get-tuple-element.21.refs_1_), channel_id=1, source_target_pairs={{0,4},{1,5},{2,6},{3,7},{4,0},{5,1},{6,2},{7,3},{8,12},{9,13},{10,... | collective-permute-start | bytes 110600 | tf_op jit(solution)/shard_map/ppermute | solution.py:427
  10.8 0.0 collective-permute-done.refs_1_
  10.8 1.6 %collective-permute-start.8 = (f32[2,64,128]{2,1,0:T(8,128)S(1)}, f32[2,64,128]{2,1,0:T(8,128)S(1)}, u32[]{:S(2)}, u32[]{:S(2)}) collective-permute-start(f32[2,64,128]{2,1,0:T(8,128)S(1)} %shard_map.51.refs_0_), channel_id=1, source_target_pairs={{0,2},{1,3},{2,0},{3,1},{4,6},{5,7},{6,4},{7,5},{8,10},{9,11},{10,... | collective-permute-start | bytes 196616 | tf_op jit(solution)/shard_map/ppermute | solution.py:427
  12.4 0.0 collective-permute-start.4
  12.4 0.2 collective-permute-done.3.refs_4_
  12.5 0.3 collective-permute-start.7
  12.9 0.9 %collective-permute-done.2.refs_3_ = f32[1,72,128]{2,1,0:T(8,128)S(1)} collective-permute-done((f32[1,72,128]{2,1,0:T(8,128)S(1)}, f32[1,72,128]{2,1,0:T(8,128)S(1)}, u32[]{:S(2)}, u32[]{:S(2)}) %collective-permute-start.2) | collective-permute-done | bytes 36896 | tf_op jit(solution)/shard_map/ppermute | solution.py:427
  13.8 0.4 %collective-permute-done.1.refs_2_ = f32[1,72,128]{2,1,0:T(8,128)S(1)} collective-permute-done((f32[1,72,128]{2,1,0:T(8,128)S(1)}, f32[1,72,128]{2,1,0:T(8,128)S(1)}, u32[]{:S(2)}, u32[]{:S(2)}) %collective-permute-start.1) | collective-permute-done | bytes 36896 | tf_op jit(solution)/shard_map/ppermute | solution.py:427
  14.2 0.1 collective-permute-start.5
  14.3 0.7 %shard_map.52 = (bf16[2,256,208]{2,1,0:T(8,128)(2,1)S(1)}, bf16[4,208,256]{2,1,0:T(8,128)(2,1)S(1)}, f32[8,128]{1,0:T(8,128)S(1)}, f32[4,128]{1,0:T(4,128)S(1)}, f32[2,4,256,256]{3,2,1,0:T(8,128)S(1)}) custom-call(f32[2,64,128]{2,1,0:T(8,128)S(1)} %shard_map.51.refs_0_, f32[1,72,128]{2,1,0:T(8,128)S(1)} %get-tuple-element.21.refs_1_, ...), custom_call_target="tpu_custom_call" | custom-call | flops 218103808 | bytes 2097152 | tf_op jit(solution)/shard_map/pallas_call | solution.py:372
  15.0 0.0 collective-permute-done.6.refs_3_
  15.1 0.4 collective-permute-done.5.refs_2_
  15.5 0.6 %shard_map.53 = (bf16[4,208,256]{2,1,0:T(8,128)(2,1)S(1)}, f32[8,128]{1,0:T(8,128)S(1)}, f32[4,128]{1,0:T(4,128)S(1)}, f32[2,4,256,256]{3,2,1,0:T(8,128)S(1)}) custom-call(bf16[2,256,208]{2,1,0:T(8,128)(2,1)S(1)} %get-tuple-element.23.refs_0_, f32[1,72,128]{2,1,0:T(8,128)S(1)} %collective-permute-done.4.refs_1_, ...), custom_call_target="tpu_custom_call" | custom-call | flops 218103808 | bytes 2097152 | tf_op jit(solution)/shard_map/pallas_call | solution.py:372
  16.1 1.0 %shard_map.54 = (f32[4,128]{1,0:T(4,128)S(1)}, f32[2,4,256,256]{3,2,1,0:T(8,128)S(1)}, f32[2,4,256,256]{3,2,1,0:T(8,128)S(1)}) custom-call(f32[2,64,128]{2,1,0:T(8,128)S(1)} %collective-permute-done.8.refs_0_, bf16[4,208,256]{2,1,0:T(8,128)(2,1)S(1)} %get-tuple-element.25.refs_1_, f32[8,128]{1,0:T(8,128)S(1)} %get-tuple-element.26.refs_2_.refs_3_, ...), custom_call_target="tpu_custom_call" | custom-call | flops 436207616 | bytes 4194304 | tf_op jit(solution)/shard_map/pallas_call | solution.py:372
  17.1 0.1 shard_map.55
  17.2 11.7 %all_to_all.10.refs_0_ = f32[32,1,1280]{2,1,0:T(1,128)S(1)} all-to-all(f32[32,1,1280]{2,1,0:T(1,128)S(1)} %shard_map.55), channel_id=1, replica_groups={{31,30,29,28,27,26,25,24,23,22,21,20,19,18,17,16,15,14,13,12,11,10,9,8,..., dimensions={0} | all-to-all | bytes 327680 | tf_op jit(solution)/shard_map/all_to_all | solution.py:383
  28.9 1.1 %shard_map.56 = (f32[32,1,384]{2,1,0:T(1,128)S(1)}, f32[5,128]{1,0:T(8,128)S(1)}) custom-call(f32[32,1,1280]{2,1,0:T(1,128)S(1)} %all_to_all.10.refs_0_, f32[2,4,256,256]{3,2,1,0:T(8,128)S(1)} %get-tuple-element.30.refs_1_, f32[2,4,256,256]{3,2,1,0:T(8,128)S(1)} %get-tuple-element.31.refs_2_, f32[2,4,256,256]{3,2,1,0:T(8,128)S(1)} %get-tuple-element.32.refs_3_, ...), custom_call_target="tpu_custom_call" | custom-call | tf_op jit(solution)/shard_map/pallas_call | solution.py:372
  30.0 9.8 %all_to_all.11.arrived = f32[32,1,384]{2,1,0:T(1,128)S(1)} all-to-all(f32[32,1,384]{2,1,0:T(1,128)S(1)} %get-tuple-element.34), channel_id=1, replica_groups={{31,30,29,28,27,26,25,24,23,22,21,20,19,18,17,16,15,14,13,12,11,10,9,8,..., dimensions={0} | all-to-all | bytes 98304 | tf_op jit(solution)/shard_map/all_to_all | solution.py:383
  39.8 0.8 %shard_map.57 = (f32[2,128]{1,0:T(2,128)}, f32[2,128]{1,0:T(2,128)}) custom-call(f32[32,1,384]{2,1,0:T(1,128)S(1)} %all_to_all.11.arrived, f32[5,128]{1,0:T(8,128)S(1)} %get-tuple-element.35.step_scalars), custom_call_target="tpu_custom_call" | custom-call | tf_op jit(solution)/shard_map/pallas_call | solution.py:372
  (6 shorter events, 0.0 us)
Async XLA Ops:
  0.6 0.7 %copy-start = (f32[256]{0:T(256)S(1)}, f32[256]{0:T(256)}, u32[]{:S(2)}) copy-start(f32[256]{0:T(256)} %param.5) | copy-start | bytes 3076
  3.2 7.6 %collective-permute-start = (f32[1,64,128]{2,1,0:T(8,128)S(1)}, f32[1,64,128]{2,1,0:T(8,128)S(1)}, u32[]{:S(2)}, u32[]{:S(2)}) collective-permute-start(f32[1,64,128]{2,1,0:T(8,128)S(1)} %get-tuple-element.20.refs_0_), channel_id=1, source_target_pairs={{0,16},{1,17},{2,18},{3,19},{4,20},{5,21},{6,22},{7,23},{8,24},{9,... | collective-permute-start | bytes 98312 | tf_op jit(solution)/shard_map/ppermute | solution.py:427
  7.3 5.2 %collective-permute-start.3 = (f32[1,72,128]{2,1,0:T(8,128)S(1)}, f32[1,72,128]{2,1,0:T(8,128)S(1)}, u32[]{:S(2)}, u32[]{:S(2)}) collective-permute-start(f32[1,72,128]{2,1,0:T(8,128)S(1)} %get-tuple-element.21.refs_1_), channel_id=1, source_target_pairs={{0,12},{1,13},{2,14},{3,15},{4,8},{5,9},{6,10},{7,11},{8,4},{9,5},... | collective-permute-start | bytes 110600 | tf_op jit(solution)/shard_map/ppermute | solution.py:427
  9.8 4.0 %collective-permute-start.2 = (f32[1,72,128]{2,1,0:T(8,128)S(1)}, f32[1,72,128]{2,1,0:T(8,128)S(1)}, u32[]{:S(2)}, u32[]{:S(2)}) collective-permute-start(f32[1,72,128]{2,1,0:T(8,128)S(1)} %get-tuple-element.21.refs_1_), channel_id=1, source_target_pairs={{0,8},{1,9},{2,10},{3,11},{4,12},{5,13},{6,14},{7,15},{8,0},{9,1},... | collective-permute-start | bytes 110600 | tf_op jit(solution)/shard_map/ppermute | solution.py:427
  10.3 4.0 %collective-permute-start.1 = (f32[1,72,128]{2,1,0:T(8,128)S(1)}, f32[1,72,128]{2,1,0:T(8,128)S(1)}, u32[]{:S(2)}, u32[]{:S(2)}) collective-permute-start(f32[1,72,128]{2,1,0:T(8,128)S(1)} %get-tuple-element.21.refs_1_), channel_id=1, source_target_pairs={{0,4},{1,5},{2,6},{3,7},{4,0},{5,1},{6,2},{7,3},{8,12},{9,13},{10,... | collective-permute-start | bytes 110600 | tf_op jit(solution)/shard_map/ppermute | solution.py:427
  10.8 5.3 %collective-permute-start.8 = (f32[2,64,128]{2,1,0:T(8,128)S(1)}, f32[2,64,128]{2,1,0:T(8,128)S(1)}, u32[]{:S(2)}, u32[]{:S(2)}) collective-permute-start(f32[2,64,128]{2,1,0:T(8,128)S(1)} %shard_map.51.refs_0_), channel_id=1, source_target_pairs={{0,2},{1,3},{2,0},{3,1},{4,6},{5,7},{6,4},{7,5},{8,10},{9,11},{10,... | collective-permute-start | bytes 196616 | tf_op jit(solution)/shard_map/ppermute | solution.py:427
  12.4 2.7 %collective-permute-start.4 = (f32[1,72,128]{2,1,0:T(8,128)S(1)}, f32[1,72,128]{2,1,0:T(8,128)S(1)}, u32[]{:S(2)}, u32[]{:S(2)}) collective-permute-start(f32[1,72,128]{2,1,0:T(8,128)S(1)} %get-tuple-element.21.refs_1_), channel_id=1, source_target_pairs={{0,1},{1,0},{2,3},{3,2},{4,5},{5,4},{6,7},{7,6},{8,9},{9,8},{10,11... | collective-permute-start | bytes 110600 | tf_op jit(solution)/shard_map/ppermute | solution.py:427
  12.5 2.5 %collective-permute-start.7 = (f32[1,72,128]{2,1,0:T(8,128)S(1)}, f32[1,72,128]{2,1,0:T(8,128)S(1)}, u32[]{:S(2)}, u32[]{:S(2)}) collective-permute-start(f32[1,72,128]{2,1,0:T(8,128)S(1)} %collective-permute-done.3.refs_4_), channel_id=1, source_target_pairs={{0,1},{1,0},{2,3},{3,2},{4,5},{5,4},{6,7},{7,6},{8,9},{9,8},{10,11... | collective-permute-start | bytes 110600 | tf_op jit(solution)/shard_map/ppermute | solution.py:427
  13.8 1.3 %collective-permute-start.6 = (f32[1,72,128]{2,1,0:T(8,128)S(1)}, f32[1,72,128]{2,1,0:T(8,128)S(1)}, u32[]{:S(2)}, u32[]{:S(2)}) collective-permute-start(f32[1,72,128]{2,1,0:T(8,128)S(1)} %collective-permute-done.2.refs_3_), channel_id=1, source_target_pairs={{0,1},{1,0},{2,3},{3,2},{4,5},{5,4},{6,7},{7,6},{8,9},{9,8},{10,11... | collective-permute-start | bytes 110600 | tf_op jit(solution)/shard_map/ppermute | solution.py:427
  14.2 1.2 %collective-permute-start.5 = (f32[1,72,128]{2,1,0:T(8,128)S(1)}, f32[1,72,128]{2,1,0:T(8,128)S(1)}, u32[]{:S(2)}, u32[]{:S(2)}) collective-permute-start(f32[1,72,128]{2,1,0:T(8,128)S(1)} %collective-permute-done.1.refs_2_), channel_id=1, source_target_pairs={{0,1},{1,0},{2,3},{3,2},{4,5},{5,4},{6,7},{7,6},{8,9},{9,8},{10,11... | collective-permute-start | bytes 110600 | tf_op jit(solution)/shard_map/ppermute | solution.py:427
where the time goes:
time: 40.9 us; the launch traced here: 40.7 us
  blocking collectives  21.5 us (53%)
  starting transfers between devices  9.55 us (23%)
  Pallas kernels  6.25 us (15%)
  waiting for transfers between devices  1.96 us (5%)
  between operations  0.68 us (2%)
  local copies, waits for them, and re-layouts  0.67 us (2%)
    all_to_all x2, blocking collectives, to_all(): lax.all_to_all(blocks, ALL, split_axis=0, concat_axis=0, axis_index_group...  21.5 us
    ppermute x9, starting transfers between devices, swap(): return lax.ppermute(value, ALL, pairs)  9.55 us
    pallas_call x8, Pallas kernels, call(): pl.pallas_call(kernel, out_shape=out_shape, scratch_shapes=list(scratch),...  6.25 us
    ppermute x9, waiting for transfers between devices, swap(): return lax.ppermute(value, ALL, pairs)  1.96 us
  transfers between devices with their start and end apart: 9, of which 4 were waited for; matrix products, arithmetic and copies ran while one was open for 0% of the time, Pallas kernels for 3%

commit v1 on v0

--- a/solution.py
+++ b/solution.py
@@ -107,47 +107,50 @@
                            preferred_element_type=f32)[0:1, :]
 
 
-def make_rows(left, right, kept, read_vector, sums, add):
+def make_rows(left, sides, sums):
     groups, rows, _ = left.shape
-    columns = right.shape[0]
     halves = rows // LANES
 
     def one_group(g, _):
         left_group = left[g]
-
-        def some_columns(step, acc):
-            first = step * TOGETHER
-            both = jnp.concatenate([right[first + k] for k in range(TOGETHER)], axis=1)
-            exponent = jnp.dot(left_group, both, preferred_element_type=f32)
-            tile = jnp.exp2(exponent)
-            for k in range(TOGETHER):
-                if kept is not None:
-                    kept[g, first + k] = tile[:, k * rows:(k + 1) * rows]
+        acc = jnp.zeros((rows, LANES), f32)
+        for right, kept, read_vector in sides:
+
+            def some_columns(step, acc):
+                first = step * TOGETHER
+                both = jnp.concatenate([right[first + k] for k in range(TOGETHER)], axis=1)
+                exponent = jnp.dot(left_group, both, preferred_element_type=f32)
+                tile = jnp.exp2(exponent)
+                for k in range(TOGETHER):
+                    if kept is not None:
+                        kept[g, first + k] = tile[:, k * rows:(k + 1) * rows]
+                    for half in range(halves):
+                        start = k * rows + half * LANES
+                        acc = acc + tile[:, start:start + LANES] * read_vector(first + k, half)
+                return acc
+
+            acc = lax.fori_loop(0, right.shape[0] // TOGETHER, some_columns, acc, unroll=4 // TOGETHER)
+        sums[g] = acc
+        return 0
+
+    lax.fori_loop(0, groups, one_group, 0, unroll=groups <= 2)
+
+
+def use_rows(sides, sums):
+    groups, rows, _ = sums.shape
+    halves = rows // LANES
+
+    def one_group(g, _):
+        acc = jnp.zeros((rows, LANES), f32)
+        for kept, read_vector in sides:
+
+            def one_column(c, acc):
                 for half in range(halves):
-                    start = k * rows + half * LANES
-                    acc = acc + tile[:, start:start + LANES] * read_vector(first + k, half)
-            return acc
-
-        start_sum = sums[g] if add else jnp.zeros((rows, LANES), f32)
-        sums[g] = lax.fori_loop(0, columns // TOGETHER, some_columns, start_sum,
-                                unroll=4 // TOGETHER)
-        return 0
-
-    lax.fori_loop(0, groups, one_group, 0, unroll=groups <= 2)
-
-
-def use_rows(kept, read_vector, sums, add):
-    groups, columns, rows, _ = kept.shape
-    halves = rows // LANES
-
-    def one_group(g, _):
-        def one_column(c, acc):
-            for half in range(halves):
-                acc = acc + kept[g, c, :, half * LANES:(half + 1) * LANES] * read_vector(c, half)
-            return acc
-
-        start_sum = sums[g] if add else jnp.zeros((rows, LANES), f32)
-        sums[g] = lax.fori_loop(0, columns, one_column, start_sum, unroll=4)
+                    acc = acc + kept[g, c, :, half * LANES:(half + 1) * LANES] * read_vector(c, half)
+                return acc
+
+            acc = lax.fori_loop(0, kept.shape[1], one_column, acc, unroll=4)
+        sums[g] = acc
         return 0
 
     lax.fori_loop(0, groups, one_group, 0, unroll=groups <= 2)
@@ -218,7 +221,7 @@
         for half in range(halves):
             line = halves * proj + half
             vector[pl.ds(source * halves + half, 1), :] = block[i, line:line + 1, :]
-    make_rows(left, right, kept, vector_reader(vector, halves), sums, False)
+    make_rows(left, [(right, kept, vector_reader(vector, halves))], sums)
     write_rows(sums, partial, [0])
 
 
@@ -231,9 +234,9 @@
         kept = (None, None)
     halves = left.shape[1] // LANES
     prepare_rows(rows_in, flips[0], left, proj, scale, wide, narrow)
-    for side in range(2):
-        right, vector = columns[2 * side:2 * side + 2]
-        make_rows(left, right, kept[side], vector_reader(vector, halves), sums, side > 0)
+    make_rows(left, [
+        (columns[2 * side], kept[side], vector_reader(columns[2 * side + 1], halves))
+        for side in range(2)], sums)
     write_rows(sums, partial, [0])
 
 
@@ -300,11 +303,10 @@
     groups = narrow // parts
     for part in range(parts):
         part_sums = sums.at[part * groups:(part + 1) * groups]
-        for side in range(2):
-            if keep:
-                use_rows(refs[1 + 2 * part + side], side_reader(side), part_sums, side > 0)
-            else:
-                make_rows(refs[3 + part], refs[1 + side], None, side_reader(side), part_sums, side > 0)
+        if keep:
+            use_rows([(refs[1 + 2 * part + side], side_reader(side)) for side in range(2)], part_sums)
+        else:
+            make_rows(refs[3 + part], [(refs[1 + side], None, side_reader(side)) for side in range(2)], part_sums)
     write_rows(sums, partial, [part_base(part, parts, wide, narrow) for part in range(parts)])
     share = jnp.zeros((1, LANES), f32)
     for r, (row_high, row_x) in enumerate(group):

time: 40.9 us -> 40.9 us (level)
  no operation moved by 1% of the time
where the time goes in v1:
time: 40.9 us; the launch traced here: 40.7 us
  blocking collectives  21.5 us (53%)
  starting transfers between devices  9.55 us (23%)
  Pallas kernels  6.25 us (15%)
  waiting for transfers between devices  1.96 us (5%)
  between operations  0.68 us (2%)
  local copies, waits for them, and re-layouts  0.67 us (2%)
    all_to_all x2, blocking collectives, to_all(): lax.all_to_all(blocks, ALL, split_axis=0, concat_axis=0, axis_index_group...  21.5 us
    ppermute x9, starting transfers between devices, swap(): return lax.ppermute(value, ALL, pairs)  9.55 us
    pallas_call x8, Pallas kernels, call(): pl.pallas_call(kernel, out_shape=out_shape, scratch_shapes=list(scratch),...  6.25 us
    ppermute x9, waiting for transfers between devices, swap(): return lax.ppermute(value, ALL, pairs)  1.96 us
  transfers between devices with their start and end apart: 9, of which 4 were waited for; matrix products, arithmetic and copies ran while one was open for 0% of the time, Pallas kernels for 3%

profile of v1, /device:TPU:0, one launch (start us, length us, event | category | flops | bytes accessed | tf_op | source)
XLA Modules:
  0.0 40.7 jit_solution(2661387371756443792)
XLA Ops:
  0.6 0.7 %copy-done = f32[256]{0:T(256)S(1)} copy-done((f32[256]{0:T(256)S(1)}, f32[256]{0:T(256)}, u32[]{:S(2)}) %copy-start) | copy-done | bytes 1048
  1.3 1.9 %shard_map.50 = (f32[1,64,128]{2,1,0:T(8,128)S(1)}, f32[1,72,128]{2,1,0:T(8,128)S(1)}) custom-call(bf16[256,2048]{1,0:T(8,128)(2,1)} %features.1, bf16[32,2048]{1,0:T(8,128)(2,1)} %bitcast.5, f32[1,256]{1,0:T(1,128)S(1)} %bitcast.4), custom_call_target="tpu_custom_call" | custom-call | tf_op jit(solution)/shard_map/pallas_call | solution.py:374
  3.2 4.1 %collective-permute-start = (f32[1,64,128]{2,1,0:T(8,128)S(1)}, f32[1,64,128]{2,1,0:T(8,128)S(1)}, u32[]{:S(2)}, u32[]{:S(2)}) collective-permute-start(f32[1,64,128]{2,1,0:T(8,128)S(1)} %get-tuple-element.20.refs_0_), channel_id=1, source_target_pairs={{0,16},{1,17},{2,18},{3,19},{4,20},{5,21},{6,22},{7,23},{8,24},{9,... | collective-permute-start | bytes 98312 | tf_op jit(solution)/shard_map/ppermute | solution.py:429
  7.3 2.5 %collective-permute-start.3 = (f32[1,72,128]{2,1,0:T(8,128)S(1)}, f32[1,72,128]{2,1,0:T(8,128)S(1)}, u32[]{:S(2)}, u32[]{:S(2)}) collective-permute-start(f32[1,72,128]{2,1,0:T(8,128)S(1)} %get-tuple-element.21.refs_1_), channel_id=1, source_target_pairs={{0,12},{1,13},{2,14},{3,15},{4,8},{5,9},{6,10},{7,11},{8,4},{9,5},... | collective-permute-start | bytes 110600 | tf_op jit(solution)/shard_map/ppermute | solution.py:429
  9.8 0.4 %collective-permute-start.2 = (f32[1,72,128]{2,1,0:T(8,128)S(1)}, f32[1,72,128]{2,1,0:T(8,128)S(1)}, u32[]{:S(2)}, u32[]{:S(2)}) collective-permute-start(f32[1,72,128]{2,1,0:T(8,128)S(1)} %get-tuple-element.21.refs_1_), channel_id=1, source_target_pairs={{0,8},{1,9},{2,10},{3,11},{4,12},{5,13},{6,14},{7,15},{8,0},{9,1},... | collective-permute-start | bytes 110600 | tf_op jit(solution)/shard_map/ppermute | solution.py:429
  10.3 0.5 %collective-permute-start.1 = (f32[1,72,128]{2,1,0:T(8,128)S(1)}, f32[1,72,128]{2,1,0:T(8,128)S(1)}, u32[]{:S(2)}, u32[]{:S(2)}) collective-permute-start(f32[1,72,128]{2,1,0:T(8,128)S(1)} %get-tuple-element.21.refs_1_), channel_id=1, source_target_pairs={{0,4},{1,5},{2,6},{3,7},{4,0},{5,1},{6,2},{7,3},{8,12},{9,13},{10,... | collective-permute-start | bytes 110600 | tf_op jit(solution)/shard_map/ppermute | solution.py:429
  10.8 0.0 collective-permute-done.refs_1_
  10.8 1.6 %collective-permute-start.8 = (f32[2,64,128]{2,1,0:T(8,128)S(1)}, f32[2,64,128]{2,1,0:T(8,128)S(1)}, u32[]{:S(2)}, u32[]{:S(2)}) collective-permute-start(f32[2,64,128]{2,1,0:T(8,128)S(1)} %shard_map.51.refs_0_), channel_id=1, source_target_pairs={{0,2},{1,3},{2,0},{3,1},{4,6},{5,7},{6,4},{7,5},{8,10},{9,11},{10,... | collective-permute-start | bytes 196616 | tf_op jit(solution)/shard_map/ppermute | solution.py:429
  12.4 0.0 collective-permute-start.4
  12.4 0.2 collective-permute-done.3.refs_4_
  12.5 0.3 collective-permute-start.7
  12.9 0.9 %collective-permute-done.2.refs_3_ = f32[1,72,128]{2,1,0:T(8,128)S(1)} collective-permute-done((f32[1,72,128]{2,1,0:T(8,128)S(1)}, f32[1,72,128]{2,1,0:T(8,128)S(1)}, u32[]{:S(2)}, u32[]{:S(2)}) %collective-permute-start.2) | collective-permute-done | bytes 36896 | tf_op jit(solution)/shard_map/ppermute | solution.py:429
  13.8 0.4 %collective-permute-done.1.refs_2_ = f32[1,72,128]{2,1,0:T(8,128)S(1)} collective-permute-done((f32[1,72,128]{2,1,0:T(8,128)S(1)}, f32[1,72,128]{2,1,0:T(8,128)S(1)}, u32[]{:S(2)}, u32[]{:S(2)}) %collective-permute-start.1) | collective-permute-done | bytes 36896 | tf_op jit(solution)/shard_map/ppermute | solution.py:429
  14.2 0.1 collective-permute-start.5
  14.3 0.7 %shard_map.52 = (bf16[2,256,208]{2,1,0:T(8,128)(2,1)S(1)}, bf16[4,208,256]{2,1,0:T(8,128)(2,1)S(1)}, f32[8,128]{1,0:T(8,128)S(1)}, f32[4,128]{1,0:T(4,128)S(1)}, f32[2,4,256,256]{3,2,1,0:T(8,128)S(1)}) custom-call(f32[2,64,128]{2,1,0:T(8,128)S(1)} %shard_map.51.refs_0_, f32[1,72,128]{2,1,0:T(8,128)S(1)} %get-tuple-element.21.refs_1_, ...), custom_call_target="tpu_custom_call" | custom-call | flops 218103808 | bytes 2097152 | tf_op jit(solution)/shard_map/pallas_call | solution.py:374
  15.0 0.0 collective-permute-done.6.refs_3_
  15.1 0.4 collective-permute-done.5.refs_2_
  15.5 0.6 %shard_map.53 = (bf16[4,208,256]{2,1,0:T(8,128)(2,1)S(1)}, f32[8,128]{1,0:T(8,128)S(1)}, f32[4,128]{1,0:T(4,128)S(1)}, f32[2,4,256,256]{3,2,1,0:T(8,128)S(1)}) custom-call(bf16[2,256,208]{2,1,0:T(8,128)(2,1)S(1)} %get-tuple-element.23.refs_0_, f32[1,72,128]{2,1,0:T(8,128)S(1)} %collective-permute-done.4.refs_1_, ...), custom_call_target="tpu_custom_call" | custom-call | flops 218103808 | bytes 2097152 | tf_op jit(solution)/shard_map/pallas_call | solution.py:374
  16.1 1.0 %shard_map.54 = (f32[4,128]{1,0:T(4,128)S(1)}, f32[2,4,256,256]{3,2,1,0:T(8,128)S(1)}, f32[2,4,256,256]{3,2,1,0:T(8,128)S(1)}) custom-call(f32[2,64,128]{2,1,0:T(8,128)S(1)} %collective-permute-done.8.refs_0_, bf16[4,208,256]{2,1,0:T(8,128)(2,1)S(1)} %get-tuple-element.25.refs_1_, f32[8,128]{1,0:T(8,128)S(1)} %get-tuple-element.26.refs_2_.refs_3_, ...), custom_call_target="tpu_custom_call" | custom-call | flops 436207616 | bytes 4194304 | tf_op jit(solution)/shard_map/pallas_call | solution.py:374
  17.1 0.1 shard_map.55
  17.2 11.7 %all_to_all.10.refs_0_ = f32[32,1,1280]{2,1,0:T(1,128)S(1)} all-to-all(f32[32,1,1280]{2,1,0:T(1,128)S(1)} %shard_map.55), channel_id=1, replica_groups={{31,30,29,28,27,26,25,24,23,22,21,20,19,18,17,16,15,14,13,12,11,10,9,8,..., dimensions={0} | all-to-all | bytes 327680 | tf_op jit(solution)/shard_map/all_to_all | solution.py:385
  28.9 1.1 %shard_map.56 = (f32[32,1,384]{2,1,0:T(1,128)S(1)}, f32[5,128]{1,0:T(8,128)S(1)}) custom-call(f32[32,1,1280]{2,1,0:T(1,128)S(1)} %all_to_all.10.refs_0_, f32[2,4,256,256]{3,2,1,0:T(8,128)S(1)} %get-tuple-element.30.refs_1_, f32[2,4,256,256]{3,2,1,0:T(8,128)S(1)} %get-tuple-element.31.refs_2_, f32[2,4,256,256]{3,2,1,0:T(8,128)S(1)} %get-tuple-element.32.refs_3_, ...), custom_call_target="tpu_custom_call" | custom-call | tf_op jit(solution)/shard_map/pallas_call | solution.py:374
  30.0 9.8 %all_to_all.11.arrived = f32[32,1,384]{2,1,0:T(1,128)S(1)} all-to-all(f32[32,1,384]{2,1,0:T(1,128)S(1)} %get-tuple-element.34), channel_id=1, replica_groups={{31,30,29,28,27,26,25,24,23,22,21,20,19,18,17,16,15,14,13,12,11,10,9,8,..., dimensions={0} | all-to-all | bytes 98304 | tf_op jit(solution)/shard_map/all_to_all | solution.py:385
  39.8 0.8 %shard_map.57 = (f32[2,128]{1,0:T(2,128)}, f32[2,128]{1,0:T(2,128)}) custom-call(f32[32,1,384]{2,1,0:T(1,128)S(1)} %all_to_all.11.arrived, f32[5,128]{1,0:T(8,128)S(1)} %get-tuple-element.35.step_scalars), custom_call_target="tpu_custom_call" | custom-call | tf_op jit(solution)/shard_map/pallas_call | solution.py:374
  (6 shorter events, 0.0 us)
Async XLA Ops:
  0.6 0.7 %copy-start = (f32[256]{0:T(256)S(1)}, f32[256]{0:T(256)}, u32[]{:S(2)}) copy-start(f32[256]{0:T(256)} %param.5) | copy-start | bytes 3076
  3.2 7.6 %collective-permute-start = (f32[1,64,128]{2,1,0:T(8,128)S(1)}, f32[1,64,128]{2,1,0:T(8,128)S(1)}, u32[]{:S(2)}, u32[]{:S(2)}) collective-permute-start(f32[1,64,128]{2,1,0:T(8,128)S(1)} %get-tuple-element.20.refs_0_), channel_id=1, source_target_pairs={{0,16},{1,17},{2,18},{3,19},{4,20},{5,21},{6,22},{7,23},{8,24},{9,... | collective-permute-start | bytes 98312 | tf_op jit(solution)/shard_map/ppermute | solution.py:429
  7.3 5.2 %collective-permute-start.3 = (f32[1,72,128]{2,1,0:T(8,128)S(1)}, f32[1,72,128]{2,1,0:T(8,128)S(1)}, u32[]{:S(2)}, u32[]{:S(2)}) collective-permute-start(f32[1,72,128]{2,1,0:T(8,128)S(1)} %get-tuple-element.21.refs_1_), channel_id=1, source_target_pairs={{0,12},{1,13},{2,14},{3,15},{4,8},{5,9},{6,10},{7,11},{8,4},{9,5},... | collective-permute-start | bytes 110600 | tf_op jit(solution)/shard_map/ppermute | solution.py:429
  9.8 4.0 %collective-permute-start.2 = (f32[1,72,128]{2,1,0:T(8,128)S(1)}, f32[1,72,128]{2,1,0:T(8,128)S(1)}, u32[]{:S(2)}, u32[]{:S(2)}) collective-permute-start(f32[1,72,128]{2,1,0:T(8,128)S(1)} %get-tuple-element.21.refs_1_), channel_id=1, source_target_pairs={{0,8},{1,9},{2,10},{3,11},{4,12},{5,13},{6,14},{7,15},{8,0},{9,1},... | collective-permute-start | bytes 110600 | tf_op jit(solution)/shard_map/ppermute | solution.py:429
  10.3 4.0 %collective-permute-start.1 = (f32[1,72,128]{2,1,0:T(8,128)S(1)}, f32[1,72,128]{2,1,0:T(8,128)S(1)}, u32[]{:S(2)}, u32[]{:S(2)}) collective-permute-start(f32[1,72,128]{2,1,0:T(8,128)S(1)} %get-tuple-element.21.refs_1_), channel_id=1, source_target_pairs={{0,4},{1,5},{2,6},{3,7},{4,0},{5,1},{6,2},{7,3},{8,12},{9,13},{10,... | collective-permute-start | bytes 110600 | tf_op jit(solution)/shard_map/ppermute | solution.py:429
  10.8 5.3 %collective-permute-start.8 = (f32[2,64,128]{2,1,0:T(8,128)S(1)}, f32[2,64,128]{2,1,0:T(8,128)S(1)}, u32[]{:S(2)}, u32[]{:S(2)}) collective-permute-start(f32[2,64,128]{2,1,0:T(8,128)S(1)} %shard_map.51.refs_0_), channel_id=1, source_target_pairs={{0,2},{1,3},{2,0},{3,1},{4,6},{5,7},{6,4},{7,5},{8,10},{9,11},{10,... | collective-permute-start | bytes 196616 | tf_op jit(solution)/shard_map/ppermute | solution.py:429
  12.4 2.7 %collective-permute-start.4 = (f32[1,72,128]{2,1,0:T(8,128)S(1)}, f32[1,72,128]{2,1,0:T(8,128)S(1)}, u32[]{:S(2)}, u32[]{:S(2)}) collective-permute-start(f32[1,72,128]{2,1,0:T(8,128)S(1)} %get-tuple-element.21.refs_1_), channel_id=1, source_target_pairs={{0,1},{1,0},{2,3},{3,2},{4,5},{5,4},{6,7},{7,6},{8,9},{9,8},{10,11... | collective-permute-start | bytes 110600 | tf_op jit(solution)/shard_map/ppermute | solution.py:429
  12.5 2.5 %collective-permute-start.7 = (f32[1,72,128]{2,1,0:T(8,128)S(1)}, f32[1,72,128]{2,1,0:T(8,128)S(1)}, u32[]{:S(2)}, u32[]{:S(2)}) collective-permute-start(f32[1,72,128]{2,1,0:T(8,128)S(1)} %collective-permute-done.3.refs_4_), channel_id=1, source_target_pairs={{0,1},{1,0},{2,3},{3,2},{4,5},{5,4},{6,7},{7,6},{8,9},{9,8},{10,11... | collective-permute-start | bytes 110600 | tf_op jit(solution)/shard_map/ppermute | solution.py:429
  13.8 1.3 %collective-permute-start.6 = (f32[1,72,128]{2,1,0:T(8,128)S(1)}, f32[1,72,128]{2,1,0:T(8,128)S(1)}, u32[]{:S(2)}, u32[]{:S(2)}) collective-permute-start(f32[1,72,128]{2,1,0:T(8,128)S(1)} %collective-permute-done.2.refs_3_), channel_id=1, source_target_pairs={{0,1},{1,0},{2,3},{3,2},{4,5},{5,4},{6,7},{7,6},{8,9},{9,8},{10,11... | collective-permute-start | bytes 110600 | tf_op jit(solution)/shard_map/ppermute | solution.py:429
  14.2 1.2 %collective-permute-start.5 = (f32[1,72,128]{2,1,0:T(8,128)S(1)}, f32[1,72,128]{2,1,0:T(8,128)S(1)}, u32[]{:S(2)}, u32[]{:S(2)}) collective-permute-start(f32[1,72,128]{2,1,0:T(8,128)S(1)} %collective-permute-done.1.refs_2_), channel_id=1, source_target_pairs={{0,1},{1,0},{2,3},{3,2},{4,5},{5,4},{6,7},{7,6},{8,9},{9,8},{10,11... | collective-permute-start | bytes 110600 | tf_op jit(solution)/shard_map/ppermute | solution.py:429

commit v2 on v0

--- a/solution.py
+++ b/solution.py
@@ -16,7 +16,6 @@
 DIRECT = 8
 KEEP_BYTES = 8 * 2**20
 VMEM_BYTES = 32 * 2**20
-WHOLE_VMEM_BYTES = (53 * 1024 + 835) * 2**10
 ALL = "all"
 HIGH, LOW, Y, X, CORE = range(5)
 highest = lax.Precision.HIGHEST
@@ -368,12 +367,12 @@
         copy.wait()
 
 
-def call(kernel, out_shape, *args, scratch=(), vmem=VMEM_BYTES, **options):
+def call(kernel, out_shape, *args, scratch=(), **options):
     return pl.pallas_call(
         kernel,
         out_shape=out_shape,
         scratch_shapes=list(scratch),
-        compiler_params=pltpu.CompilerParams(vmem_limit_bytes=vmem),
+        compiler_params=pltpu.CompilerParams(vmem_limit_bytes=VMEM_BYTES),
         **options,
     )(*args)
 
@@ -449,9 +448,11 @@
         return pltpu.VMEM(dims, dtype)
 
     feat = features.shape[1]
+    inputs = [pltpu.with_memory_space_constraint(value, pltpu.HBM)
+              for value in (features, projection.T, targets.reshape(1, rows))]
     latent, own = call(
-        project_kernel, (shape(1, halves * proj, LANES), shape(1, halves * proj + 8, LANES)), features, projection.T, targets.reshape(1, rows),
-        in_specs=[pl.BlockSpec(memory_space=pl.ANY)] * 3, vmem=WHOLE_VMEM_BYTES,
+        project_kernel, (shape(1, halves * proj, LANES), shape(1, halves * proj + 8, LANES)), *inputs,
+        in_specs=[pl.BlockSpec(memory_space=pltpu.HBM)] * 3,
         scratch=[scratch(halves, LANES, feat, dtype=bf16), scratch(proj, feat, dtype=bf16),
                  scratch(1, rows), pltpu.SemaphoreType.DMA((halves + 2,))])
     row_parts, sides, flips = first_round(latent, own, wide, narrow)

time: 40.9 us -> 40.2 us (0.983)
  local copies, waits for them, and re-layouts: 0.67 us -> 0 us
    unnamed x2 -> x0, local copies, waits for them, and re-layouts: 0.67 us -> none
where the time goes in v2:
time: 40.2 us; the launch traced here: 40 us
  blocking collectives  21.5 us (53%)
  starting transfers between devices  9.55 us (24%)
  Pallas kernels  6.25 us (16%)
  waiting for transfers between devices  1.97 us (5%)
  between operations  0.68 us (2%)
    all_to_all x2, blocking collectives, to_all(): lax.all_to_all(blocks, ALL, split_axis=0, concat_axis=0, axis_index_group...  21.5 us
    ppermute x9, starting transfers between devices, swap(): return lax.ppermute(value, ALL, pairs)  9.55 us
    pallas_call x8, Pallas kernels, call(): pl.pallas_call(kernel, out_shape=out_shape, scratch_shapes=list(scratch),...  6.25 us
    ppermute x9, waiting for transfers between devices, swap(): return lax.ppermute(value, ALL, pairs)  1.97 us
  transfers between devices with their start and end apart: 9, of which 4 were waited for; matrix products, arithmetic and copies ran while one was open for 0% of the time, Pallas kernels for 3%

profile of v2, /device:TPU:0, one launch (start us, length us, event | category | flops | bytes accessed | tf_op | source)
XLA Modules:
  0.0 40.0 jit_solution(4490841714890302160)
XLA Ops:
  0.6 1.9 %shard_map.50 = (f32[1,64,128]{2,1,0:T(8,128)S(1)}, f32[1,72,128]{2,1,0:T(8,128)S(1)}) custom-call(bf16[256,2048]{1,0:T(8,128)(2,1)} %features.1, bf16[32,2048]{1,0:T(8,128)(2,1)} %bitcast.4, f32[1,256]{1,0:T(1,128)} %bitcast.5), custom_call_target="tpu_custom_call" | custom-call | tf_op jit(solution)/shard_map/pallas_call | solution.py:371
  2.5 4.1 %collective-permute-start = (f32[1,64,128]{2,1,0:T(8,128)S(1)}, f32[1,64,128]{2,1,0:T(8,128)S(1)}, u32[]{:S(2)}, u32[]{:S(2)}) collective-permute-start(f32[1,64,128]{2,1,0:T(8,128)S(1)} %get-tuple-element.20.refs_0_), channel_id=1, source_target_pairs={{0,16},{1,17},{2,18},{3,19},{4,20},{5,21},{6,22},{7,23},{8,24},{9,... | collective-permute-start | bytes 98312 | tf_op jit(solution)/shard_map/ppermute | solution.py:426
  6.6 2.5 %collective-permute-start.3 = (f32[1,72,128]{2,1,0:T(8,128)S(1)}, f32[1,72,128]{2,1,0:T(8,128)S(1)}, u32[]{:S(2)}, u32[]{:S(2)}) collective-permute-start(f32[1,72,128]{2,1,0:T(8,128)S(1)} %get-tuple-element.21.refs_1_), channel_id=1, source_target_pairs={{0,12},{1,13},{2,14},{3,15},{4,8},{5,9},{6,10},{7,11},{8,4},{9,5},... | collective-permute-start | bytes 110600 | tf_op jit(solution)/shard_map/ppermute | solution.py:426
  9.2 0.4 %collective-permute-start.2 = (f32[1,72,128]{2,1,0:T(8,128)S(1)}, f32[1,72,128]{2,1,0:T(8,128)S(1)}, u32[]{:S(2)}, u32[]{:S(2)}) collective-permute-start(f32[1,72,128]{2,1,0:T(8,128)S(1)} %get-tuple-element.21.refs_1_), channel_id=1, source_target_pairs={{0,8},{1,9},{2,10},{3,11},{4,12},{5,13},{6,14},{7,15},{8,0},{9,1},... | collective-permute-start | bytes 110600 | tf_op jit(solution)/shard_map/ppermute | solution.py:426
  9.6 0.5 %collective-permute-start.1 = (f32[1,72,128]{2,1,0:T(8,128)S(1)}, f32[1,72,128]{2,1,0:T(8,128)S(1)}, u32[]{:S(2)}, u32[]{:S(2)}) collective-permute-start(f32[1,72,128]{2,1,0:T(8,128)S(1)} %get-tuple-element.21.refs_1_), channel_id=1, source_target_pairs={{0,4},{1,5},{2,6},{3,7},{4,0},{5,1},{6,2},{7,3},{8,12},{9,13},{10,... | collective-permute-start | bytes 110600 | tf_op jit(solution)/shard_map/ppermute | solution.py:426
  10.1 1.6 %collective-permute-start.8 = (f32[2,64,128]{2,1,0:T(8,128)S(1)}, f32[2,64,128]{2,1,0:T(8,128)S(1)}, u32[]{:S(2)}, u32[]{:S(2)}) collective-permute-start(f32[2,64,128]{2,1,0:T(8,128)S(1)} %shard_map.51.refs_0_), channel_id=1, source_target_pairs={{0,2},{1,3},{2,0},{3,1},{4,6},{5,7},{6,4},{7,5},{8,10},{9,11},{10,... | collective-permute-start | bytes 196616 | tf_op jit(solution)/shard_map/ppermute | solution.py:426
  11.7 0.2 collective-permute-done.3.refs_4_
  11.9 0.3 collective-permute-start.7
  12.2 0.9 %collective-permute-done.2.refs_3_ = f32[1,72,128]{2,1,0:T(8,128)S(1)} collective-permute-done((f32[1,72,128]{2,1,0:T(8,128)S(1)}, f32[1,72,128]{2,1,0:T(8,128)S(1)}, u32[]{:S(2)}, u32[]{:S(2)}) %collective-permute-start.2) | collective-permute-done | bytes 36896 | tf_op jit(solution)/shard_map/ppermute | solution.py:426
  13.1 0.4 %collective-permute-done.1.refs_2_ = f32[1,72,128]{2,1,0:T(8,128)S(1)} collective-permute-done((f32[1,72,128]{2,1,0:T(8,128)S(1)}, f32[1,72,128]{2,1,0:T(8,128)S(1)}, u32[]{:S(2)}, u32[]{:S(2)}) %collective-permute-start.1) | collective-permute-done | bytes 36896 | tf_op jit(solution)/shard_map/ppermute | solution.py:426
  13.6 0.1 collective-permute-start.5
  13.6 0.7 %shard_map.52 = (bf16[2,256,208]{2,1,0:T(8,128)(2,1)S(1)}, bf16[4,208,256]{2,1,0:T(8,128)(2,1)S(1)}, f32[8,128]{1,0:T(8,128)S(1)}, f32[4,128]{1,0:T(4,128)S(1)}, f32[2,4,256,256]{3,2,1,0:T(8,128)S(1)}) custom-call(f32[2,64,128]{2,1,0:T(8,128)S(1)} %shard_map.51.refs_0_, f32[1,72,128]{2,1,0:T(8,128)S(1)} %get-tuple-element.21.refs_1_, ...), custom_call_target="tpu_custom_call" | custom-call | flops 218103808 | bytes 2097152 | tf_op jit(solution)/shard_map/pallas_call | solution.py:371
  14.4 0.0 collective-permute-done.4.refs_1_
  14.4 0.0 collective-permute-done.7.refs_4_
  14.4 0.0 collective-permute-done.6.refs_3_
  14.4 0.4 collective-permute-done.5.refs_2_
  14.8 0.6 %shard_map.53 = (bf16[4,208,256]{2,1,0:T(8,128)(2,1)S(1)}, f32[8,128]{1,0:T(8,128)S(1)}, f32[4,128]{1,0:T(4,128)S(1)}, f32[2,4,256,256]{3,2,1,0:T(8,128)S(1)}) custom-call(bf16[2,256,208]{2,1,0:T(8,128)(2,1)S(1)} %get-tuple-element.23.refs_0_, f32[1,72,128]{2,1,0:T(8,128)S(1)} %collective-permute-done.4.refs_1_, ...), custom_call_target="tpu_custom_call" | custom-call | flops 218103808 | bytes 2097152 | tf_op jit(solution)/shard_map/pallas_call | solution.py:371
  15.4 0.0 collective-permute-done.8.refs_0_
  15.4 1.0 %shard_map.54 = (f32[4,128]{1,0:T(4,128)S(1)}, f32[2,4,256,256]{3,2,1,0:T(8,128)S(1)}, f32[2,4,256,256]{3,2,1,0:T(8,128)S(1)}) custom-call(f32[2,64,128]{2,1,0:T(8,128)S(1)} %collective-permute-done.8.refs_0_, bf16[4,208,256]{2,1,0:T(8,128)(2,1)S(1)} %get-tuple-element.25.refs_1_, f32[8,128]{1,0:T(8,128)S(1)} %get-tuple-element.26.refs_2_.refs_3_, ...), custom_call_target="tpu_custom_call" | custom-call | flops 436207616 | bytes 4194304 | tf_op jit(solution)/shard_map/pallas_call | solution.py:371
  16.4 0.1 shard_map.55
  16.5 11.7 %all_to_all.10.refs_0_ = f32[32,1,1280]{2,1,0:T(1,128)S(1)} all-to-all(f32[32,1,1280]{2,1,0:T(1,128)S(1)} %shard_map.55), channel_id=1, replica_groups={{31,30,29,28,27,26,25,24,23,22,21,20,19,18,17,16,15,14,13,12,11,10,9,8,..., dimensions={0} | all-to-all | bytes 327680 | tf_op jit(solution)/shard_map/all_to_all | solution.py:382
  28.2 1.1 %shard_map.56 = (f32[32,1,384]{2,1,0:T(1,128)S(1)}, f32[5,128]{1,0:T(8,128)S(1)}) custom-call(f32[32,1,1280]{2,1,0:T(1,128)S(1)} %all_to_all.10.refs_0_, f32[2,4,256,256]{3,2,1,0:T(8,128)S(1)} %get-tuple-element.30.refs_1_, f32[2,4,256,256]{3,2,1,0:T(8,128)S(1)} %get-tuple-element.31.refs_2_, f32[2,4,256,256]{3,2,1,0:T(8,128)S(1)} %get-tuple-element.32.refs_3_, ...), custom_call_target="tpu_custom_call" | custom-call | tf_op jit(solution)/shard_map/pallas_call | solution.py:371
  29.3 9.8 %all_to_all.11.arrived = f32[32,1,384]{2,1,0:T(1,128)S(1)} all-to-all(f32[32,1,384]{2,1,0:T(1,128)S(1)} %get-tuple-element.34), channel_id=1, replica_groups={{31,30,29,28,27,26,25,24,23,22,21,20,19,18,17,16,15,14,13,12,11,10,9,8,..., dimensions={0} | all-to-all | bytes 98304 | tf_op jit(solution)/shard_map/all_to_all | solution.py:382
  39.1 0.8 %shard_map.57 = (f32[2,128]{1,0:T(2,128)}, f32[2,128]{1,0:T(2,128)}) custom-call(f32[32,1,384]{2,1,0:T(1,128)S(1)} %all_to_all.11.arrived, f32[5,128]{1,0:T(8,128)S(1)} %get-tuple-element.35.step_scalars), custom_call_target="tpu_custom_call" | custom-call | tf_op jit(solution)/shard_map/pallas_call | solution.py:371
  (4 shorter events, 0.0 us)
Async XLA Ops:
  2.5 7.6 %collective-permute-start = (f32[1,64,128]{2,1,0:T(8,128)S(1)}, f32[1,64,128]{2,1,0:T(8,128)S(1)}, u32[]{:S(2)}, u32[]{:S(2)}) collective-permute-start(f32[1,64,128]{2,1,0:T(8,128)S(1)} %get-tuple-element.20.refs_0_), channel_id=1, source_target_pairs={{0,16},{1,17},{2,18},{3,19},{4,20},{5,21},{6,22},{7,23},{8,24},{9,... | collective-permute-start | bytes 98312 | tf_op jit(solution)/shard_map/ppermute | solution.py:426
  6.6 5.2 %collective-permute-start.3 = (f32[1,72,128]{2,1,0:T(8,128)S(1)}, f32[1,72,128]{2,1,0:T(8,128)S(1)}, u32[]{:S(2)}, u32[]{:S(2)}) collective-permute-start(f32[1,72,128]{2,1,0:T(8,128)S(1)} %get-tuple-element.21.refs_1_), channel_id=1, source_target_pairs={{0,12},{1,13},{2,14},{3,15},{4,8},{5,9},{6,10},{7,11},{8,4},{9,5},... | collective-permute-start | bytes 110600 | tf_op jit(solution)/shard_map/ppermute | solution.py:426
  9.2 4.0 %collective-permute-start.2 = (f32[1,72,128]{2,1,0:T(8,128)S(1)}, f32[1,72,128]{2,1,0:T(8,128)S(1)}, u32[]{:S(2)}, u32[]{:S(2)}) collective-permute-start(f32[1,72,128]{2,1,0:T(8,128)S(1)} %get-tuple-element.21.refs_1_), channel_id=1, source_target_pairs={{0,8},{1,9},{2,10},{3,11},{4,12},{5,13},{6,14},{7,15},{8,0},{9,1},... | collective-permute-start | bytes 110600 | tf_op jit(solution)/shard_map/ppermute | solution.py:426
  9.6 4.0 %collective-permute-start.1 = (f32[1,72,128]{2,1,0:T(8,128)S(1)}, f32[1,72,128]{2,1,0:T(8,128)S(1)}, u32[]{:S(2)}, u32[]{:S(2)}) collective-permute-start(f32[1,72,128]{2,1,0:T(8,128)S(1)} %get-tuple-element.21.refs_1_), channel_id=1, source_target_pairs={{0,4},{1,5},{2,6},{3,7},{4,0},{5,1},{6,2},{7,3},{8,12},{9,13},{10,... | collective-permute-start | bytes 110600 | tf_op jit(solution)/shard_map/ppermute | solution.py:426
  10.1 5.3 %collective-permute-start.8 = (f32[2,64,128]{2,1,0:T(8,128)S(1)}, f32[2,64,128]{2,1,0:T(8,128)S(1)}, u32[]{:S(2)}, u32[]{:S(2)}) collective-permute-start(f32[2,64,128]{2,1,0:T(8,128)S(1)} %shard_map.51.refs_0_), channel_id=1, source_target_pairs={{0,2},{1,3},{2,0},{3,1},{4,6},{5,7},{6,4},{7,5},{8,10},{9,11},{10,... | collective-permute-start | bytes 196616 | tf_op jit(solution)/shard_map/ppermute | solution.py:426
  11.7 2.7 %collective-permute-start.4 = (f32[1,72,128]{2,1,0:T(8,128)S(1)}, f32[1,72,128]{2,1,0:T(8,128)S(1)}, u32[]{:S(2)}, u32[]{:S(2)}) collective-permute-start(f32[1,72,128]{2,1,0:T(8,128)S(1)} %get-tuple-element.21.refs_1_), channel_id=1, source_target_pairs={{0,1},{1,0},{2,3},{3,2},{4,5},{5,4},{6,7},{7,6},{8,9},{9,8},{10,11... | collective-permute-start | bytes 110600 | tf_op jit(solution)/shard_map/ppermute | solution.py:426
  11.9 2.5 %collective-permute-start.7 = (f32[1,72,128]{2,1,0:T(8,128)S(1)}, f32[1,72,128]{2,1,0:T(8,128)S(1)}, u32[]{:S(2)}, u32[]{:S(2)}) collective-permute-start(f32[1,72,128]{2,1,0:T(8,128)S(1)} %collective-permute-done.3.refs_4_), channel_id=1, source_target_pairs={{0,1},{1,0},{2,3},{3,2},{4,5},{5,4},{6,7},{7,6},{8,9},{9,8},{10,11... | collective-permute-start | bytes 110600 | tf_op jit(solution)/shard_map/ppermute | solution.py:426
  13.1 1.3 %collective-permute-start.6 = (f32[1,72,128]{2,1,0:T(8,128)S(1)}, f32[1,72,128]{2,1,0:T(8,128)S(1)}, u32[]{:S(2)}, u32[]{:S(2)}) collective-permute-start(f32[1,72,128]{2,1,0:T(8,128)S(1)} %collective-permute-done.2.refs_3_), channel_id=1, source_target_pairs={{0,1},{1,0},{2,3},{3,2},{4,5},{5,4},{6,7},{7,6},{8,9},{9,8},{10,11... | collective-permute-start | bytes 110600 | tf_op jit(solution)/shard_map/ppermute | solution.py:426
  13.6 1.2 %collective-permute-start.5 = (f32[1,72,128]{2,1,0:T(8,128)S(1)}, f32[1,72,128]{2,1,0:T(8,128)S(1)}, u32[]{:S(2)}, u32[]{:S(2)}) collective-permute-start(f32[1,72,128]{2,1,0:T(8,128)S(1)} %collective-permute-done.1.refs_2_), channel_id=1, source_target_pairs={{0,1},{1,0},{2,3},{3,2},{4,5},{5,4},{6,7},{7,6},{8,9},{9,8},{10,11... | collective-permute-start | bytes 110600 | tf_op jit(solution)/shard_map/ppermute | solution.py:426

commit v3 on v1

--- a/solution.py
+++ b/solution.py
@@ -16,7 +16,6 @@
 DIRECT = 8
 KEEP_BYTES = 8 * 2**20
 VMEM_BYTES = 32 * 2**20
-WHOLE_VMEM_BYTES = (53 * 1024 + 835) * 2**10
 ALL = "all"
 HIGH, LOW, Y, X, CORE = range(5)
 highest = lax.Precision.HIGHEST
@@ -174,11 +173,11 @@
     copies = [
         pltpu.make_async_copy(features.at[pl.ds(i * height, height)], feature_buf.at[i], sems.at[i])
         for i in range(chunks)]
-    copies.insert(1, pltpu.make_async_copy(projection_t, projection_buf, sems.at[chunks]))
+    copies.insert(0, pltpu.make_async_copy(projection_t, projection_buf, sems.at[chunks]))
     copies.append(pltpu.make_async_copy(targets, target_buf, sems.at[chunks + 1]))
     for copy in copies:
         copy.start()
-    copies.pop(1).wait()
+    copies.pop(0).wait()
     for i in range(chunks):
         copies[i].wait()
         some = lax.dot_general(
@@ -226,11 +225,11 @@
 
 
 def rest_kernel(proj, scale, wide, narrow, keep, flips, *refs):
-    rows_in, columns, refs = refs[:1], refs[1:5], refs[5:]
+    rows_in, columns, earlier, refs = refs[:1], refs[1:5], refs[5:7], refs[7:]
     if keep:
-        partial, *kept, sums, left = refs
+        out, *kept, sums, partial, held, left = refs
     else:
-        left, partial, sums = refs
+        left, out, sums, partial, held = refs
         kept = (None, None)
     halves = left.shape[1] // LANES
     prepare_rows(rows_in, flips[0], left, proj, scale, wide, narrow)
@@ -238,6 +237,7 @@
         (columns[2 * side], kept[side], vector_reader(columns[2 * side + 1], halves))
         for side in range(2)], sums)
     write_rows(sums, partial, [0])
+    message_kernel(2, wide, narrow, halves, *earlier, partial, columns[1], out, held)
 
 
 def message_kernel(parts, wide, narrow, halves, *refs):
@@ -370,12 +370,12 @@
         copy.wait()
 
 
-def call(kernel, out_shape, *args, scratch=(), vmem=VMEM_BYTES, **options):
+def call(kernel, out_shape, *args, scratch=(), **options):
     return pl.pallas_call(
         kernel,
         out_shape=out_shape,
         scratch_shapes=list(scratch),
-        compiler_params=pltpu.CompilerParams(vmem_limit_bytes=vmem),
+        compiler_params=pltpu.CompilerParams(vmem_limit_bytes=VMEM_BYTES),
         **options,
     )(*args)
 
@@ -451,9 +451,11 @@
         return pltpu.VMEM(dims, dtype)
 
     feat = features.shape[1]
+    inputs = [pltpu.with_memory_space_constraint(value, pltpu.HBM)
+              for value in (features, projection.T, targets.reshape(1, rows))]
     latent, own = call(
-        project_kernel, (shape(1, halves * proj, LANES), shape(1, halves * proj + 8, LANES)), features, projection.T, targets.reshape(1, rows),
-        in_specs=[pl.BlockSpec(memory_space=pl.ANY)] * 3, vmem=WHOLE_VMEM_BYTES,
+        project_kernel, (shape(1, halves * proj, LANES), shape(1, halves * proj + 8, LANES)), *inputs,
+        in_specs=[pl.BlockSpec(memory_space=pltpu.HBM)] * 3,
         scratch=[scratch(halves, LANES, feat, dtype=bf16), scratch(proj, feat, dtype=bf16),
                  scratch(1, rows), pltpu.SemaphoreType.DMA((halves + 2,))])
     row_parts, sides, flips = first_round(latent, own, wide, narrow)
@@ -483,20 +485,21 @@
         columns += made[:2]
         partials.append(made[2])
         blocks += made[3:]
-    for row_blocks in row_parts[1:]:
+    message = shape(devices, 1, (lines + halves) * LANES)
+    if parts == 2:
         made = call(
             functools.partial(rest_kernel, *settings),
-            (group_lines, *kept * 2) if keep else (left, group_lines), *row_blocks, *columns,
-            scratch=[sums, scratch(*left.shape, dtype=bf16)] if keep else [sums],
+            (message, *kept * 2) if keep else (left, message), *row_parts[1], *columns, *partials,
+            scratch=[sums, scratch(groups * halves, LANES), scratch(lines, LANES)]
+            + ([scratch(*left.shape, dtype=bf16)] if keep else []),
             cost_estimate=cost(wide))
-        if not keep:
-            lefts.append(made[0])
-        partials.append(made[0 if keep else 1])
+        out = made[0 if keep else 1]
         blocks += made[1:] if keep else []
-    out = call(
-        functools.partial(message_kernel, parts, wide, narrow, halves),
-        shape(devices, 1, (lines + halves) * LANES), *partials, columns[1],
-        scratch=[scratch(lines, LANES)])
+        lefts += [] if keep else made[:1]
+    else:
+        out = call(
+            functools.partial(message_kernel, parts, wide, narrow, halves), message,
+            *partials, columns[1], scratch=[scratch(lines, LANES)])
     block = blocks if keep else [columns[0], columns[2], *lefts]
     sums = scratch(narrow, rows, LANES)
     out, step_scalars = call(

time: 40.9 us -> 40.2 us (0.983)
  local copies, waits for them, and re-layouts: 0.67 us -> 0 us
    unnamed x2 -> x0, local copies, waits for them, and re-layouts: 0.67 us -> none
    pallas_call x8 -> x7, Pallas kernels: 6.25 us -> 6.27 us  [call(): pl.pallas_call(kernel, out_shape=out_shape, scratch_shapes=list(scratch),...]
where the time goes in v3:
time: 40.2 us; the launch traced here: 40 us
  blocking collectives  21.5 us (53%)
  starting transfers between devices  9.55 us (24%)
  Pallas kernels  6.27 us (16%)
  waiting for transfers between devices  1.97 us (5%)
  between operations  0.68 us (2%)
    all_to_all x2, blocking collectives, to_all(): lax.all_to_all(blocks, ALL, split_axis=0, concat_axis=0, axis_index_group...  21.5 us
    ppermute x9, starting transfers between devices, swap(): return lax.ppermute(value, ALL, pairs)  9.55 us
    pallas_call x7, Pallas kernels, call(): pl.pallas_call(kernel, out_shape=out_shape, scratch_shapes=list(scratch),...  6.27 us
    ppermute x9, waiting for transfers between devices, swap(): return lax.ppermute(value, ALL, pairs)  1.97 us
  transfers between devices with their start and end apart: 9, of which 4 were waited for; matrix products, arithmetic and copies ran while one was open for 0% of the time, Pallas kernels for 3%

profile of v3, /device:TPU:0, one launch (start us, length us, event | category | flops | bytes accessed | tf_op | source)
XLA Modules:
  0.0 40.0 jit_solution(16305927054042694877)
XLA Ops:
  0.6 1.9 %shard_map.50 = (f32[1,64,128]{2,1,0:T(8,128)S(1)}, f32[1,72,128]{2,1,0:T(8,128)S(1)}) custom-call(bf16[256,2048]{1,0:T(8,128)(2,1)} %features.1, bf16[32,2048]{1,0:T(8,128)(2,1)} %bitcast.4, f32[1,256]{1,0:T(1,128)} %bitcast.5), custom_call_target="tpu_custom_call" | custom-call | tf_op jit(solution)/shard_map/pallas_call | solution.py:374
  2.6 4.1 %collective-permute-start = (f32[1,64,128]{2,1,0:T(8,128)S(1)}, f32[1,64,128]{2,1,0:T(8,128)S(1)}, u32[]{:S(2)}, u32[]{:S(2)}) collective-permute-start(f32[1,64,128]{2,1,0:T(8,128)S(1)} %get-tuple-element.20.refs_0_), channel_id=1, source_target_pairs={{0,16},{1,17},{2,18},{3,19},{4,20},{5,21},{6,22},{7,23},{8,24},{9,... | collective-permute-start | bytes 98312 | tf_op jit(solution)/shard_map/ppermute | solution.py:429
  6.7 2.5 %collective-permute-start.4 = (f32[1,72,128]{2,1,0:T(8,128)S(1)}, f32[1,72,128]{2,1,0:T(8,128)S(1)}, u32[]{:S(2)}, u32[]{:S(2)}) collective-permute-start(f32[1,72,128]{2,1,0:T(8,128)S(1)} %get-tuple-element.21.refs_1_), channel_id=1, source_target_pairs={{0,12},{1,13},{2,14},{3,15},{4,8},{5,9},{6,10},{7,11},{8,4},{9,5},... | collective-permute-start | bytes 110600 | tf_op jit(solution)/shard_map/ppermute | solution.py:429
  9.2 0.4 %collective-permute-start.3 = (f32[1,72,128]{2,1,0:T(8,128)S(1)}, f32[1,72,128]{2,1,0:T(8,128)S(1)}, u32[]{:S(2)}, u32[]{:S(2)}) collective-permute-start(f32[1,72,128]{2,1,0:T(8,128)S(1)} %get-tuple-element.21.refs_1_), channel_id=1, source_target_pairs={{0,8},{1,9},{2,10},{3,11},{4,12},{5,13},{6,14},{7,15},{8,0},{9,1},... | collective-permute-start | bytes 110600 | tf_op jit(solution)/shard_map/ppermute | solution.py:429
  9.7 0.5 %collective-permute-start.2 = (f32[1,72,128]{2,1,0:T(8,128)S(1)}, f32[1,72,128]{2,1,0:T(8,128)S(1)}, u32[]{:S(2)}, u32[]{:S(2)}) collective-permute-start(f32[1,72,128]{2,1,0:T(8,128)S(1)} %get-tuple-element.21.refs_1_), channel_id=1, source_target_pairs={{0,4},{1,5},{2,6},{3,7},{4,0},{5,1},{6,2},{7,3},{8,12},{9,13},{10,... | collective-permute-start | bytes 110600 | tf_op jit(solution)/shard_map/ppermute | solution.py:429
  10.2 0.0 collective-permute-done.refs_1_
  10.2 1.6 %collective-permute-start.1 = (f32[2,64,128]{2,1,0:T(8,128)S(1)}, f32[2,64,128]{2,1,0:T(8,128)S(1)}, u32[]{:S(2)}, u32[]{:S(2)}) collective-permute-start(f32[2,64,128]{2,1,0:T(8,128)S(1)} %shard_map.51.refs_0_), channel_id=1, source_target_pairs={{0,2},{1,3},{2,0},{3,1},{4,6},{5,7},{6,4},{7,5},{8,10},{9,11},{10,... | collective-permute-start | bytes 196616 | tf_op jit(solution)/shard_map/ppermute | solution.py:429
  11.7 0.0 collective-permute-start.5
  11.7 0.2 collective-permute-done.4.refs_4_
  11.9 0.3 collective-permute-start.8
  12.3 0.9 %collective-permute-done.3.refs_3_ = f32[1,72,128]{2,1,0:T(8,128)S(1)} collective-permute-done((f32[1,72,128]{2,1,0:T(8,128)S(1)}, f32[1,72,128]{2,1,0:T(8,128)S(1)}, u32[]{:S(2)}, u32[]{:S(2)}) %collective-permute-start.3) | collective-permute-done | bytes 36896 | tf_op jit(solution)/shard_map/ppermute | solution.py:429
  13.2 0.0 collective-permute-start.7
  13.2 0.4 %collective-permute-done.2.refs_2_ = f32[1,72,128]{2,1,0:T(8,128)S(1)} collective-permute-done((f32[1,72,128]{2,1,0:T(8,128)S(1)}, f32[1,72,128]{2,1,0:T(8,128)S(1)}, u32[]{:S(2)}, u32[]{:S(2)}) %collective-permute-start.2) | collective-permute-done | bytes 36896 | tf_op jit(solution)/shard_map/ppermute | solution.py:429
  13.6 0.1 collective-permute-start.6
  13.7 0.7 %shard_map.52 = (bf16[2,256,208]{2,1,0:T(8,128)(2,1)S(1)}, bf16[4,208,256]{2,1,0:T(8,128)(2,1)S(1)}, f32[8,128]{1,0:T(8,128)S(1)}, f32[4,128]{1,0:T(4,128)S(1)}, f32[2,4,256,256]{3,2,1,0:T(8,128)S(1)}) custom-call(f32[2,64,128]{2,1,0:T(8,128)S(1)} %shard_map.51.refs_0_, f32[1,72,128]{2,1,0:T(8,128)S(1)} %get-tuple-element.21.refs_1_, ...), custom_call_target="tpu_custom_call" | custom-call | flops 218103808 | bytes 2097152 | tf_op jit(solution)/shard_map/pallas_call | solution.py:374
  14.4 0.0 collective-permute-done.5.refs_1_
  14.4 0.0 collective-permute-done.7.refs_3_
  14.4 0.4 collective-permute-done.6.refs_2_
  14.8 0.6 %shard_map.53 = (bf16[4,208,256]{2,1,0:T(8,128)(2,1)S(1)}, f32[8,128]{1,0:T(8,128)S(1)}, f32[4,128]{1,0:T(4,128)S(1)}, f32[2,4,256,256]{3,2,1,0:T(8,128)S(1)}) custom-call(bf16[2,256,208]{2,1,0:T(8,128)(2,1)S(1)} %get-tuple-element.24.refs_0_, f32[1,72,128]{2,1,0:T(8,128)S(1)} %collective-permute-done.5.refs_1_, ...), custom_call_target="tpu_custom_call" | custom-call | flops 218103808 | bytes 2097152 | tf_op jit(solution)/shard_map/pallas_call | solution.py:374
  15.5 1.1 %shard_map.54 = (f32[32,1,1280]{2,1,0:T(1,128)S(1)}, f32[2,4,256,256]{3,2,1,0:T(8,128)S(1)}, f32[2,4,256,256]{3,2,1,0:T(8,128)S(1)}) custom-call(f32[2,64,128]{2,1,0:T(8,128)S(1)} %collective-permute-done.1.refs_0_, bf16[4,208,256]{2,1,0:T(8,128)(2,1)S(1)} %get-tuple-element.22.refs_1_, f32[8,128]{1,0:T(8,128)S(1)} %get-tuple-element.23.refs_2_, ...), custom_call_target="tpu_custom_call" | custom-call | flops 436207616 | bytes 4194304 | tf_op jit(solution)/shard_map/pallas_call | solution.py:374
  16.6 11.7 %all_to_all.10.refs_0_ = f32[32,1,1280]{2,1,0:T(1,128)S(1)} all-to-all(f32[32,1,1280]{2,1,0:T(1,128)S(1)} %get-tuple-element.29), channel_id=1, replica_groups={{31,30,29,28,27,26,25,24,23,22,21,20,19,18,17,16,15,14,13,12,11,10,9,8,..., dimensions={0} | all-to-all | bytes 327680 | tf_op jit(solution)/shard_map/all_to_all | solution.py:385
  28.3 1.1 %shard_map.55 = (f32[32,1,384]{2,1,0:T(1,128)S(1)}, f32[5,128]{1,0:T(8,128)S(1)}) custom-call(f32[32,1,1280]{2,1,0:T(1,128)S(1)} %all_to_all.10.refs_0_, f32[2,4,256,256]{3,2,1,0:T(8,128)S(1)} %get-tuple-element.30.refs_1_, f32[2,4,256,256]{3,2,1,0:T(8,128)S(1)} %get-tuple-element.31.refs_2_, f32[2,4,256,256]{3,2,1,0:T(8,128)S(1)} %get-tuple-element.32.refs_3_, ...), custom_call_target="tpu_custom_call" | custom-call | tf_op jit(solution)/shard_map/pallas_call | solution.py:374
  29.4 9.8 %all_to_all.11.arrived = f32[32,1,384]{2,1,0:T(1,128)S(1)} all-to-all(f32[32,1,384]{2,1,0:T(1,128)S(1)} %get-tuple-element.34), channel_id=1, replica_groups={{31,30,29,28,27,26,25,24,23,22,21,20,19,18,17,16,15,14,13,12,11,10,9,8,..., dimensions={0} | all-to-all | bytes 98304 | tf_op jit(solution)/shard_map/all_to_all | solution.py:385
  39.2 0.8 %shard_map.56 = (f32[2,128]{1,0:T(2,128)}, f32[2,128]{1,0:T(2,128)}) custom-call(f32[32,1,384]{2,1,0:T(1,128)S(1)} %all_to_all.11.arrived, f32[5,128]{1,0:T(8,128)S(1)} %get-tuple-element.35.step_scalars), custom_call_target="tpu_custom_call" | custom-call | tf_op jit(solution)/shard_map/pallas_call | solution.py:374
  (3 shorter events, 0.0 us)
Async XLA Ops:
  2.6 7.6 %collective-permute-start = (f32[1,64,128]{2,1,0:T(8,128)S(1)}, f32[1,64,128]{2,1,0:T(8,128)S(1)}, u32[]{:S(2)}, u32[]{:S(2)}) collective-permute-start(f32[1,64,128]{2,1,0:T(8,128)S(1)} %get-tuple-element.20.refs_0_), channel_id=1, source_target_pairs={{0,16},{1,17},{2,18},{3,19},{4,20},{5,21},{6,22},{7,23},{8,24},{9,... | collective-permute-start | bytes 98312 | tf_op jit(solution)/shard_map/ppermute | solution.py:429
  6.7 5.2 %collective-permute-start.4 = (f32[1,72,128]{2,1,0:T(8,128)S(1)}, f32[1,72,128]{2,1,0:T(8,128)S(1)}, u32[]{:S(2)}, u32[]{:S(2)}) collective-permute-start(f32[1,72,128]{2,1,0:T(8,128)S(1)} %get-tuple-element.21.refs_1_), channel_id=1, source_target_pairs={{0,12},{1,13},{2,14},{3,15},{4,8},{5,9},{6,10},{7,11},{8,4},{9,5},... | collective-permute-start | bytes 110600 | tf_op jit(solution)/shard_map/ppermute | solution.py:429
  9.2 4.0 %collective-permute-start.3 = (f32[1,72,128]{2,1,0:T(8,128)S(1)}, f32[1,72,128]{2,1,0:T(8,128)S(1)}, u32[]{:S(2)}, u32[]{:S(2)}) collective-permute-start(f32[1,72,128]{2,1,0:T(8,128)S(1)} %get-tuple-element.21.refs_1_), channel_id=1, source_target_pairs={{0,8},{1,9},{2,10},{3,11},{4,12},{5,13},{6,14},{7,15},{8,0},{9,1},... | collective-permute-start | bytes 110600 | tf_op jit(solution)/shard_map/ppermute | solution.py:429
  9.7 4.0 %collective-permute-start.2 = (f32[1,72,128]{2,1,0:T(8,128)S(1)}, f32[1,72,128]{2,1,0:T(8,128)S(1)}, u32[]{:S(2)}, u32[]{:S(2)}) collective-permute-start(f32[1,72,128]{2,1,0:T(8,128)S(1)} %get-tuple-element.21.refs_1_), channel_id=1, source_target_pairs={{0,4},{1,5},{2,6},{3,7},{4,0},{5,1},{6,2},{7,3},{8,12},{9,13},{10,... | collective-permute-start | bytes 110600 | tf_op jit(solution)/shard_map/ppermute | solution.py:429
  10.2 5.3 %collective-permute-start.1 = (f32[2,64,128]{2,1,0:T(8,128)S(1)}, f32[2,64,128]{2,1,0:T(8,128)S(1)}, u32[]{:S(2)}, u32[]{:S(2)}) collective-permute-start(f32[2,64,128]{2,1,0:T(8,128)S(1)} %shard_map.51.refs_0_), channel_id=1, source_target_pairs={{0,2},{1,3},{2,0},{3,1},{4,6},{5,7},{6,4},{7,5},{8,10},{9,11},{10,... | collective-permute-start | bytes 196616 | tf_op jit(solution)/shard_map/ppermute | solution.py:429
  11.7 2.7 %collective-permute-start.5 = (f32[1,72,128]{2,1,0:T(8,128)S(1)}, f32[1,72,128]{2,1,0:T(8,128)S(1)}, u32[]{:S(2)}, u32[]{:S(2)}) collective-permute-start(f32[1,72,128]{2,1,0:T(8,128)S(1)} %get-tuple-element.21.refs_1_), channel_id=1, source_target_pairs={{0,1},{1,0},{2,3},{3,2},{4,5},{5,4},{6,7},{7,6},{8,9},{9,8},{10,11... | collective-permute-start | bytes 110600 | tf_op jit(solution)/shard_map/ppermute | solution.py:429
  11.9 2.5 %collective-permute-start.8 = (f32[1,72,128]{2,1,0:T(8,128)S(1)}, f32[1,72,128]{2,1,0:T(8,128)S(1)}, u32[]{:S(2)}, u32[]{:S(2)}) collective-permute-start(f32[1,72,128]{2,1,0:T(8,128)S(1)} %collective-permute-done.4.refs_4_), channel_id=1, source_target_pairs={{0,1},{1,0},{2,3},{3,2},{4,5},{5,4},{6,7},{7,6},{8,9},{9,8},{10,11... | collective-permute-start | bytes 110600 | tf_op jit(solution)/shard_map/ppermute | solution.py:429
  13.2 1.3 %collective-permute-start.7 = (f32[1,72,128]{2,1,0:T(8,128)S(1)}, f32[1,72,128]{2,1,0:T(8,128)S(1)}, u32[]{:S(2)}, u32[]{:S(2)}) collective-permute-start(f32[1,72,128]{2,1,0:T(8,128)S(1)} %collective-permute-done.3.refs_3_), channel_id=1, source_target_pairs={{0,1},{1,0},{2,3},{3,2},{4,5},{5,4},{6,7},{7,6},{8,9},{9,8},{10,11... | collective-permute-start | bytes 110600 | tf_op jit(solution)/shard_map/ppermute | solution.py:429
  13.6 1.2 %collective-permute-start.6 = (f32[1,72,128]{2,1,0:T(8,128)S(1)}, f32[1,72,128]{2,1,0:T(8,128)S(1)}, u32[]{:S(2)}, u32[]{:S(2)}) collective-permute-start(f32[1,72,128]{2,1,0:T(8,128)S(1)} %collective-permute-done.2.refs_2_), channel_id=1, source_target_pairs={{0,1},{1,0},{2,3},{3,2},{4,5},{5,4},{6,7},{7,6},{8,9},{9,8},{10,11... | collective-permute-start | bytes 110600 | tf_op jit(solution)/shard_map/ppermute | solution.py:429

commit v4 on v3

--- a/solution.py
+++ b/solution.py
@@ -173,11 +173,11 @@
     copies = [
         pltpu.make_async_copy(features.at[pl.ds(i * height, height)], feature_buf.at[i], sems.at[i])
         for i in range(chunks)]
-    copies.insert(0, pltpu.make_async_copy(projection_t, projection_buf, sems.at[chunks]))
+    copies.insert(1, pltpu.make_async_copy(projection_t, projection_buf, sems.at[chunks]))
     copies.append(pltpu.make_async_copy(targets, target_buf, sems.at[chunks + 1]))
     for copy in copies:
         copy.start()
-    copies.pop(0).wait()
+    copies.pop(1).wait()
     for i in range(chunks):
         copies[i].wait()
         some = lax.dot_general(

time: 40.2 us -> 40.1 us (level)
  no operation moved by 1% of the time
where the time goes in v4:
time: 40.1 us; the launch traced here: 40 us
  blocking collectives  21.5 us (54%)
  starting transfers between devices  9.55 us (24%)
  Pallas kernels  6.22 us (16%)
  waiting for transfers between devices  1.97 us (5%)
  between operations  0.68 us (2%)
    all_to_all x2, blocking collectives, to_all(): lax.all_to_all(blocks, ALL, split_axis=0, concat_axis=0, axis_index_group...  21.5 us
    ppermute x9, starting transfers between devices, swap(): return lax.ppermute(value, ALL, pairs)  9.55 us
    pallas_call x7, Pallas kernels, call(): pl.pallas_call(kernel, out_shape=out_shape, scratch_shapes=list(scratch),...  6.22 us
    ppermute x9, waiting for transfers between devices, swap(): return lax.ppermute(value, ALL, pairs)  1.97 us
  transfers between devices with their start and end apart: 9, of which 4 were waited for; matrix products, arithmetic and copies ran while one was open for 0% of the time, Pallas kernels for 3%

profile of v4, /device:TPU:0, one launch (start us, length us, event | category | flops | bytes accessed | tf_op | source)
XLA Modules:
  0.0 40.0 jit_solution(9412204259911757102)
XLA Ops:
  0.6 1.9 %shard_map.50 = (f32[1,64,128]{2,1,0:T(8,128)S(1)}, f32[1,72,128]{2,1,0:T(8,128)S(1)}) custom-call(bf16[256,2048]{1,0:T(8,128)(2,1)} %features.1, bf16[32,2048]{1,0:T(8,128)(2,1)} %bitcast.4, f32[1,256]{1,0:T(1,128)} %bitcast.5), custom_call_target="tpu_custom_call" | custom-call | tf_op jit(solution)/shard_map/pallas_call | solution.py:374
  2.5 4.1 %collective-permute-start = (f32[1,64,128]{2,1,0:T(8,128)S(1)}, f32[1,64,128]{2,1,0:T(8,128)S(1)}, u32[]{:S(2)}, u32[]{:S(2)}) collective-permute-start(f32[1,64,128]{2,1,0:T(8,128)S(1)} %get-tuple-element.20.refs_0_), channel_id=1, source_target_pairs={{0,16},{1,17},{2,18},{3,19},{4,20},{5,21},{6,22},{7,23},{8,24},{9,... | collective-permute-start | bytes 98312 | tf_op jit(solution)/shard_map/ppermute | solution.py:429
  6.6 2.5 %collective-permute-start.4 = (f32[1,72,128]{2,1,0:T(8,128)S(1)}, f32[1,72,128]{2,1,0:T(8,128)S(1)}, u32[]{:S(2)}, u32[]{:S(2)}) collective-permute-start(f32[1,72,128]{2,1,0:T(8,128)S(1)} %get-tuple-element.21.refs_1_), channel_id=1, source_target_pairs={{0,12},{1,13},{2,14},{3,15},{4,8},{5,9},{6,10},{7,11},{8,4},{9,5},... | collective-permute-start | bytes 110600 | tf_op jit(solution)/shard_map/ppermute | solution.py:429
  9.2 0.4 %collective-permute-start.3 = (f32[1,72,128]{2,1,0:T(8,128)S(1)}, f32[1,72,128]{2,1,0:T(8,128)S(1)}, u32[]{:S(2)}, u32[]{:S(2)}) collective-permute-start(f32[1,72,128]{2,1,0:T(8,128)S(1)} %get-tuple-element.21.refs_1_), channel_id=1, source_target_pairs={{0,8},{1,9},{2,10},{3,11},{4,12},{5,13},{6,14},{7,15},{8,0},{9,1},... | collective-permute-start | bytes 110600 | tf_op jit(solution)/shard_map/ppermute | solution.py:429
  9.6 0.5 %collective-permute-start.2 = (f32[1,72,128]{2,1,0:T(8,128)S(1)}, f32[1,72,128]{2,1,0:T(8,128)S(1)}, u32[]{:S(2)}, u32[]{:S(2)}) collective-permute-start(f32[1,72,128]{2,1,0:T(8,128)S(1)} %get-tuple-element.21.refs_1_), channel_id=1, source_target_pairs={{0,4},{1,5},{2,6},{3,7},{4,0},{5,1},{6,2},{7,3},{8,12},{9,13},{10,... | collective-permute-start | bytes 110600 | tf_op jit(solution)/shard_map/ppermute | solution.py:429
  10.1 0.0 collective-permute-done.refs_1_
  10.1 1.6 %collective-permute-start.1 = (f32[2,64,128]{2,1,0:T(8,128)S(1)}, f32[2,64,128]{2,1,0:T(8,128)S(1)}, u32[]{:S(2)}, u32[]{:S(2)}) collective-permute-start(f32[2,64,128]{2,1,0:T(8,128)S(1)} %shard_map.51.refs_0_), channel_id=1, source_target_pairs={{0,2},{1,3},{2,0},{3,1},{4,6},{5,7},{6,4},{7,5},{8,10},{9,11},{10,... | collective-permute-start | bytes 196616 | tf_op jit(solution)/shard_map/ppermute | solution.py:429
  11.7 0.0 collective-permute-start.5
  11.7 0.2 collective-permute-done.4.refs_4_
  11.9 0.3 collective-permute-start.8
  12.2 0.9 %collective-permute-done.3.refs_3_ = f32[1,72,128]{2,1,0:T(8,128)S(1)} collective-permute-done((f32[1,72,128]{2,1,0:T(8,128)S(1)}, f32[1,72,128]{2,1,0:T(8,128)S(1)}, u32[]{:S(2)}, u32[]{:S(2)}) %collective-permute-start.3) | collective-permute-done | bytes 36896 | tf_op jit(solution)/shard_map/ppermute | solution.py:429
  13.1 0.0 collective-permute-start.7
  13.1 0.4 %collective-permute-done.2.refs_2_ = f32[1,72,128]{2,1,0:T(8,128)S(1)} collective-permute-done((f32[1,72,128]{2,1,0:T(8,128)S(1)}, f32[1,72,128]{2,1,0:T(8,128)S(1)}, u32[]{:S(2)}, u32[]{:S(2)}) %collective-permute-start.2) | collective-permute-done | bytes 36896 | tf_op jit(solution)/shard_map/ppermute | solution.py:429
  13.6 0.1 collective-permute-start.6
  13.6 0.7 %shard_map.52 = (bf16[2,256,208]{2,1,0:T(8,128)(2,1)S(1)}, bf16[4,208,256]{2,1,0:T(8,128)(2,1)S(1)}, f32[8,128]{1,0:T(8,128)S(1)}, f32[4,128]{1,0:T(4,128)S(1)}, f32[2,4,256,256]{3,2,1,0:T(8,128)S(1)}) custom-call(f32[2,64,128]{2,1,0:T(8,128)S(1)} %shard_map.51.refs_0_, f32[1,72,128]{2,1,0:T(8,128)S(1)} %get-tuple-element.21.refs_1_, ...), custom_call_target="tpu_custom_call" | custom-call | flops 218103808 | bytes 2097152 | tf_op jit(solution)/shard_map/pallas_call | solution.py:374
  14.4 0.0 collective-permute-done.7.refs_3_
  14.4 0.4 collective-permute-done.6.refs_2_
  14.8 0.6 %shard_map.53 = (bf16[4,208,256]{2,1,0:T(8,128)(2,1)S(1)}, f32[8,128]{1,0:T(8,128)S(1)}, f32[4,128]{1,0:T(4,128)S(1)}, f32[2,4,256,256]{3,2,1,0:T(8,128)S(1)}) custom-call(bf16[2,256,208]{2,1,0:T(8,128)(2,1)S(1)} %get-tuple-element.24.refs_0_, f32[1,72,128]{2,1,0:T(8,128)S(1)} %collective-permute-done.5.refs_1_, ...), custom_call_target="tpu_custom_call" | custom-call | flops 218103808 | bytes 2097152 | tf_op jit(solution)/shard_map/pallas_call | solution.py:374
  15.4 0.0 collective-permute-done.1.refs_0_
  15.4 1.1 %shard_map.54 = (f32[32,1,1280]{2,1,0:T(1,128)S(1)}, f32[2,4,256,256]{3,2,1,0:T(8,128)S(1)}, f32[2,4,256,256]{3,2,1,0:T(8,128)S(1)}) custom-call(f32[2,64,128]{2,1,0:T(8,128)S(1)} %collective-permute-done.1.refs_0_, bf16[4,208,256]{2,1,0:T(8,128)(2,1)S(1)} %get-tuple-element.22.refs_1_, f32[8,128]{1,0:T(8,128)S(1)} %get-tuple-element.23.refs_2_, ...), custom_call_target="tpu_custom_call" | custom-call | flops 436207616 | bytes 4194304 | tf_op jit(solution)/shard_map/pallas_call | solution.py:374
  16.5 11.7 %all_to_all.10.refs_0_ = f32[32,1,1280]{2,1,0:T(1,128)S(1)} all-to-all(f32[32,1,1280]{2,1,0:T(1,128)S(1)} %get-tuple-element.29), channel_id=1, replica_groups={{31,30,29,28,27,26,25,24,23,22,21,20,19,18,17,16,15,14,13,12,11,10,9,8,..., dimensions={0} | all-to-all | bytes 327680 | tf_op jit(solution)/shard_map/all_to_all | solution.py:385
  28.2 1.1 %shard_map.55 = (f32[32,1,384]{2,1,0:T(1,128)S(1)}, f32[5,128]{1,0:T(8,128)S(1)}) custom-call(f32[32,1,1280]{2,1,0:T(1,128)S(1)} %all_to_all.10.refs_0_, f32[2,4,256,256]{3,2,1,0:T(8,128)S(1)} %get-tuple-element.30.refs_1_, f32[2,4,256,256]{3,2,1,0:T(8,128)S(1)} %get-tuple-element.31.refs_2_, f32[2,4,256,256]{3,2,1,0:T(8,128)S(1)} %get-tuple-element.32.refs_3_, ...), custom_call_target="tpu_custom_call" | custom-call | tf_op jit(solution)/shard_map/pallas_call | solution.py:374
  29.3 9.8 %all_to_all.11.arrived = f32[32,1,384]{2,1,0:T(1,128)S(1)} all-to-all(f32[32,1,384]{2,1,0:T(1,128)S(1)} %get-tuple-element.34), channel_id=1, replica_groups={{31,30,29,28,27,26,25,24,23,22,21,20,19,18,17,16,15,14,13,12,11,10,9,8,..., dimensions={0} | all-to-all | bytes 98304 | tf_op jit(solution)/shard_map/all_to_all | solution.py:385
  39.1 0.8 %shard_map.56 = (f32[2,128]{1,0:T(2,128)}, f32[2,128]{1,0:T(2,128)}) custom-call(f32[32,1,384]{2,1,0:T(1,128)S(1)} %all_to_all.11.arrived, f32[5,128]{1,0:T(8,128)S(1)} %get-tuple-element.35.step_scalars), custom_call_target="tpu_custom_call" | custom-call | tf_op jit(solution)/shard_map/pallas_call | solution.py:374
  (3 shorter events, 0.0 us)
Async XLA Ops:
  2.5 7.6 %collective-permute-start = (f32[1,64,128]{2,1,0:T(8,128)S(1)}, f32[1,64,128]{2,1,0:T(8,128)S(1)}, u32[]{:S(2)}, u32[]{:S(2)}) collective-permute-start(f32[1,64,128]{2,1,0:T(8,128)S(1)} %get-tuple-element.20.refs_0_), channel_id=1, source_target_pairs={{0,16},{1,17},{2,18},{3,19},{4,20},{5,21},{6,22},{7,23},{8,24},{9,... | collective-permute-start | bytes 98312 | tf_op jit(solution)/shard_map/ppermute | solution.py:429
  6.6 5.2 %collective-permute-start.4 = (f32[1,72,128]{2,1,0:T(8,128)S(1)}, f32[1,72,128]{2,1,0:T(8,128)S(1)}, u32[]{:S(2)}, u32[]{:S(2)}) collective-permute-start(f32[1,72,128]{2,1,0:T(8,128)S(1)} %get-tuple-element.21.refs_1_), channel_id=1, source_target_pairs={{0,12},{1,13},{2,14},{3,15},{4,8},{5,9},{6,10},{7,11},{8,4},{9,5},... | collective-permute-start | bytes 110600 | tf_op jit(solution)/shard_map/ppermute | solution.py:429
  9.2 4.0 %collective-permute-start.3 = (f32[1,72,128]{2,1,0:T(8,128)S(1)}, f32[1,72,128]{2,1,0:T(8,128)S(1)}, u32[]{:S(2)}, u32[]{:S(2)}) collective-permute-start(f32[1,72,128]{2,1,0:T(8,128)S(1)} %get-tuple-element.21.refs_1_), channel_id=1, source_target_pairs={{0,8},{1,9},{2,10},{3,11},{4,12},{5,13},{6,14},{7,15},{8,0},{9,1},... | collective-permute-start | bytes 110600 | tf_op jit(solution)/shard_map/ppermute | solution.py:429
  9.6 4.0 %collective-permute-start.2 = (f32[1,72,128]{2,1,0:T(8,128)S(1)}, f32[1,72,128]{2,1,0:T(8,128)S(1)}, u32[]{:S(2)}, u32[]{:S(2)}) collective-permute-start(f32[1,72,128]{2,1,0:T(8,128)S(1)} %get-tuple-element.21.refs_1_), channel_id=1, source_target_pairs={{0,4},{1,5},{2,6},{3,7},{4,0},{5,1},{6,2},{7,3},{8,12},{9,13},{10,... | collective-permute-start | bytes 110600 | tf_op jit(solution)/shard_map/ppermute | solution.py:429
  10.1 5.3 %collective-permute-start.1 = (f32[2,64,128]{2,1,0:T(8,128)S(1)}, f32[2,64,128]{2,1,0:T(8,128)S(1)}, u32[]{:S(2)}, u32[]{:S(2)}) collective-permute-start(f32[2,64,128]{2,1,0:T(8,128)S(1)} %shard_map.51.refs_0_), channel_id=1, source_target_pairs={{0,2},{1,3},{2,0},{3,1},{4,6},{5,7},{6,4},{7,5},{8,10},{9,11},{10,... | collective-permute-start | bytes 196616 | tf_op jit(solution)/shard_map/ppermute | solution.py:429
  11.7 2.7 %collective-permute-start.5 = (f32[1,72,128]{2,1,0:T(8,128)S(1)}, f32[1,72,128]{2,1,0:T(8,128)S(1)}, u32[]{:S(2)}, u32[]{:S(2)}) collective-permute-start(f32[1,72,128]{2,1,0:T(8,128)S(1)} %get-tuple-element.21.refs_1_), channel_id=1, source_target_pairs={{0,1},{1,0},{2,3},{3,2},{4,5},{5,4},{6,7},{7,6},{8,9},{9,8},{10,11... | collective-permute-start | bytes 110600 | tf_op jit(solution)/shard_map/ppermute | solution.py:429
  11.9 2.5 %collective-permute-start.8 = (f32[1,72,128]{2,1,0:T(8,128)S(1)}, f32[1,72,128]{2,1,0:T(8,128)S(1)}, u32[]{:S(2)}, u32[]{:S(2)}) collective-permute-start(f32[1,72,128]{2,1,0:T(8,128)S(1)} %collective-permute-done.4.refs_4_), channel_id=1, source_target_pairs={{0,1},{1,0},{2,3},{3,2},{4,5},{5,4},{6,7},{7,6},{8,9},{9,8},{10,11... | collective-permute-start | bytes 110600 | tf_op jit(solution)/shard_map/ppermute | solution.py:429
  13.1 1.3 %collective-permute-start.7 = (f32[1,72,128]{2,1,0:T(8,128)S(1)}, f32[1,72,128]{2,1,0:T(8,128)S(1)}, u32[]{:S(2)}, u32[]{:S(2)}) collective-permute-start(f32[1,72,128]{2,1,0:T(8,128)S(1)} %collective-permute-done.3.refs_3_), channel_id=1, source_target_pairs={{0,1},{1,0},{2,3},{3,2},{4,5},{5,4},{6,7},{7,6},{8,9},{9,8},{10,11... | collective-permute-start | bytes 110600 | tf_op jit(solution)/shard_map/ppermute | solution.py:429
  13.6 1.2 %collective-permute-start.6 = (f32[1,72,128]{2,1,0:T(8,128)S(1)}, f32[1,72,128]{2,1,0:T(8,128)S(1)}, u32[]{:S(2)}, u32[]{:S(2)}) collective-permute-start(f32[1,72,128]{2,1,0:T(8,128)S(1)} %collective-permute-done.2.refs_2_), channel_id=1, source_target_pairs={{0,1},{1,0},{2,3},{3,2},{4,5},{5,4},{6,7},{7,6},{8,9},{9,8},{10,11... | collective-permute-start | bytes 110600 | tf_op jit(solution)/shard_map/ppermute | solution.py:429

commit v5 on v4

--- a/solution.py
+++ b/solution.py
@@ -11,7 +11,7 @@
 
 noise_var = 0.5
 LANES = 128
-TOGETHER = 2
+TOGETHER = 4
 EARLY = 10**9
 DIRECT = 8
 KEEP_BYTES = 8 * 2**20

time: 40.1 us -> 40.1 us (level)
  no operation moved by 1% of the time
where the time goes in v5:
time: 40.1 us; the launch traced here: 40 us
  blocking collectives  21.5 us (54%)
  starting transfers between devices  9.55 us (24%)
  Pallas kernels  6.22 us (16%)
  waiting for transfers between devices  1.97 us (5%)
  between operations  0.68 us (2%)
    all_to_all x2, blocking collectives, to_all(): lax.all_to_all(blocks, ALL, split_axis=0, concat_axis=0, axis_index_group...  21.5 us
    ppermute x9, starting transfers between devices, swap(): return lax.ppermute(value, ALL, pairs)  9.55 us
    pallas_call x7, Pallas kernels, call(): pl.pallas_call(kernel, out_shape=out_shape, scratch_shapes=list(scratch),...  6.22 us
    ppermute x9, waiting for transfers between devices, swap(): return lax.ppermute(value, ALL, pairs)  1.97 us
  transfers between devices with their start and end apart: 9, of which 4 were waited for; matrix products, arithmetic and copies ran while one was open for 0% of the time, Pallas kernels for 3%

profile of v5, /device:TPU:0, one launch (start us, length us, event | category | flops | bytes accessed | tf_op | source)
XLA Modules:
  0.0 40.0 jit_solution(9412204259911757102)
XLA Ops:
  0.6 1.9 %shard_map.50 = (f32[1,64,128]{2,1,0:T(8,128)S(1)}, f32[1,72,128]{2,1,0:T(8,128)S(1)}) custom-call(bf16[256,2048]{1,0:T(8,128)(2,1)} %features.1, bf16[32,2048]{1,0:T(8,128)(2,1)} %bitcast.4, f32[1,256]{1,0:T(1,128)} %bitcast.5), custom_call_target="tpu_custom_call" | custom-call | tf_op jit(solution)/shard_map/pallas_call | solution.py:374
  2.5 4.1 %collective-permute-start = (f32[1,64,128]{2,1,0:T(8,128)S(1)}, f32[1,64,128]{2,1,0:T(8,128)S(1)}, u32[]{:S(2)}, u32[]{:S(2)}) collective-permute-start(f32[1,64,128]{2,1,0:T(8,128)S(1)} %get-tuple-element.20.refs_0_), channel_id=1, source_target_pairs={{0,16},{1,17},{2,18},{3,19},{4,20},{5,21},{6,22},{7,23},{8,24},{9,... | collective-permute-start | bytes 98312 | tf_op jit(solution)/shard_map/ppermute | solution.py:429
  6.6 2.5 %collective-permute-start.4 = (f32[1,72,128]{2,1,0:T(8,128)S(1)}, f32[1,72,128]{2,1,0:T(8,128)S(1)}, u32[]{:S(2)}, u32[]{:S(2)}) collective-permute-start(f32[1,72,128]{2,1,0:T(8,128)S(1)} %get-tuple-element.21.refs_1_), channel_id=1, source_target_pairs={{0,12},{1,13},{2,14},{3,15},{4,8},{5,9},{6,10},{7,11},{8,4},{9,5},... | collective-permute-start | bytes 110600 | tf_op jit(solution)/shard_map/ppermute | solution.py:429
  9.2 0.4 %collective-permute-start.3 = (f32[1,72,128]{2,1,0:T(8,128)S(1)}, f32[1,72,128]{2,1,0:T(8,128)S(1)}, u32[]{:S(2)}, u32[]{:S(2)}) collective-permute-start(f32[1,72,128]{2,1,0:T(8,128)S(1)} %get-tuple-element.21.refs_1_), channel_id=1, source_target_pairs={{0,8},{1,9},{2,10},{3,11},{4,12},{5,13},{6,14},{7,15},{8,0},{9,1},... | collective-permute-start | bytes 110600 | tf_op jit(solution)/shard_map/ppermute | solution.py:429
  9.6 0.5 %collective-permute-start.2 = (f32[1,72,128]{2,1,0:T(8,128)S(1)}, f32[1,72,128]{2,1,0:T(8,128)S(1)}, u32[]{:S(2)}, u32[]{:S(2)}) collective-permute-start(f32[1,72,128]{2,1,0:T(8,128)S(1)} %get-tuple-element.21.refs_1_), channel_id=1, source_target_pairs={{0,4},{1,5},{2,6},{3,7},{4,0},{5,1},{6,2},{7,3},{8,12},{9,13},{10,... | collective-permute-start | bytes 110600 | tf_op jit(solution)/shard_map/ppermute | solution.py:429
  10.1 0.0 collective-permute-done.refs_1_
  10.1 1.6 %collective-permute-start.1 = (f32[2,64,128]{2,1,0:T(8,128)S(1)}, f32[2,64,128]{2,1,0:T(8,128)S(1)}, u32[]{:S(2)}, u32[]{:S(2)}) collective-permute-start(f32[2,64,128]{2,1,0:T(8,128)S(1)} %shard_map.51.refs_0_), channel_id=1, source_target_pairs={{0,2},{1,3},{2,0},{3,1},{4,6},{5,7},{6,4},{7,5},{8,10},{9,11},{10,... | collective-permute-start | bytes 196616 | tf_op jit(solution)/shard_map/ppermute | solution.py:429
  11.7 0.0 collective-permute-start.5
  11.7 0.2 collective-permute-done.4.refs_4_
  11.9 0.3 collective-permute-start.8
  12.2 0.9 %collective-permute-done.3.refs_3_ = f32[1,72,128]{2,1,0:T(8,128)S(1)} collective-permute-done((f32[1,72,128]{2,1,0:T(8,128)S(1)}, f32[1,72,128]{2,1,0:T(8,128)S(1)}, u32[]{:S(2)}, u32[]{:S(2)}) %collective-permute-start.3) | collective-permute-done | bytes 36896 | tf_op jit(solution)/shard_map/ppermute | solution.py:429
  13.1 0.0 collective-permute-start.7
  13.1 0.4 %collective-permute-done.2.refs_2_ = f32[1,72,128]{2,1,0:T(8,128)S(1)} collective-permute-done((f32[1,72,128]{2,1,0:T(8,128)S(1)}, f32[1,72,128]{2,1,0:T(8,128)S(1)}, u32[]{:S(2)}, u32[]{:S(2)}) %collective-permute-start.2) | collective-permute-done | bytes 36896 | tf_op jit(solution)/shard_map/ppermute | solution.py:429
  13.6 0.1 collective-permute-start.6
  13.6 0.7 %shard_map.52 = (bf16[2,256,208]{2,1,0:T(8,128)(2,1)S(1)}, bf16[4,208,256]{2,1,0:T(8,128)(2,1)S(1)}, f32[8,128]{1,0:T(8,128)S(1)}, f32[4,128]{1,0:T(4,128)S(1)}, f32[2,4,256,256]{3,2,1,0:T(8,128)S(1)}) custom-call(f32[2,64,128]{2,1,0:T(8,128)S(1)} %shard_map.51.refs_0_, f32[1,72,128]{2,1,0:T(8,128)S(1)} %get-tuple-element.21.refs_1_, ...), custom_call_target="tpu_custom_call" | custom-call | flops 218103808 | bytes 2097152 | tf_op jit(solution)/shard_map/pallas_call | solution.py:374
  14.4 0.0 collective-permute-done.7.refs_3_
  14.4 0.4 collective-permute-done.6.refs_2_
  14.8 0.6 %shard_map.53 = (bf16[4,208,256]{2,1,0:T(8,128)(2,1)S(1)}, f32[8,128]{1,0:T(8,128)S(1)}, f32[4,128]{1,0:T(4,128)S(1)}, f32[2,4,256,256]{3,2,1,0:T(8,128)S(1)}) custom-call(bf16[2,256,208]{2,1,0:T(8,128)(2,1)S(1)} %get-tuple-element.24.refs_0_, f32[1,72,128]{2,1,0:T(8,128)S(1)} %collective-permute-done.5.refs_1_, ...), custom_call_target="tpu_custom_call" | custom-call | flops 218103808 | bytes 2097152 | tf_op jit(solution)/shard_map/pallas_call | solution.py:374
  15.4 0.0 collective-permute-done.1.refs_0_
  15.4 1.1 %shard_map.54 = (f32[32,1,1280]{2,1,0:T(1,128)S(1)}, f32[2,4,256,256]{3,2,1,0:T(8,128)S(1)}, f32[2,4,256,256]{3,2,1,0:T(8,128)S(1)}) custom-call(f32[2,64,128]{2,1,0:T(8,128)S(1)} %collective-permute-done.1.refs_0_, bf16[4,208,256]{2,1,0:T(8,128)(2,1)S(1)} %get-tuple-element.22.refs_1_, f32[8,128]{1,0:T(8,128)S(1)} %get-tuple-element.23.refs_2_, ...), custom_call_target="tpu_custom_call" | custom-call | flops 436207616 | bytes 4194304 | tf_op jit(solution)/shard_map/pallas_call | solution.py:374
  16.5 11.7 %all_to_all.10.refs_0_ = f32[32,1,1280]{2,1,0:T(1,128)S(1)} all-to-all(f32[32,1,1280]{2,1,0:T(1,128)S(1)} %get-tuple-element.29), channel_id=1, replica_groups={{31,30,29,28,27,26,25,24,23,22,21,20,19,18,17,16,15,14,13,12,11,10,9,8,..., dimensions={0} | all-to-all | bytes 327680 | tf_op jit(solution)/shard_map/all_to_all | solution.py:385
  28.2 1.1 %shard_map.55 = (f32[32,1,384]{2,1,0:T(1,128)S(1)}, f32[5,128]{1,0:T(8,128)S(1)}) custom-call(f32[32,1,1280]{2,1,0:T(1,128)S(1)} %all_to_all.10.refs_0_, f32[2,4,256,256]{3,2,1,0:T(8,128)S(1)} %get-tuple-element.30.refs_1_, f32[2,4,256,256]{3,2,1,0:T(8,128)S(1)} %get-tuple-element.31.refs_2_, f32[2,4,256,256]{3,2,1,0:T(8,128)S(1)} %get-tuple-element.32.refs_3_, ...), custom_call_target="tpu_custom_call" | custom-call | tf_op jit(solution)/shard_map/pallas_call | solution.py:374
  29.3 9.8 %all_to_all.11.arrived = f32[32,1,384]{2,1,0:T(1,128)S(1)} all-to-all(f32[32,1,384]{2,1,0:T(1,128)S(1)} %get-tuple-element.34), channel_id=1, replica_groups={{31,30,29,28,27,26,25,24,23,22,21,20,19,18,17,16,15,14,13,12,11,10,9,8,..., dimensions={0} | all-to-all | bytes 98304 | tf_op jit(solution)/shard_map/all_to_all | solution.py:385
  39.1 0.8 %shard_map.56 = (f32[2,128]{1,0:T(2,128)}, f32[2,128]{1,0:T(2,128)}) custom-call(f32[32,1,384]{2,1,0:T(1,128)S(1)} %all_to_all.11.arrived, f32[5,128]{1,0:T(8,128)S(1)} %get-tuple-element.35.step_scalars), custom_call_target="tpu_custom_call" | custom-call | tf_op jit(solution)/shard_map/pallas_call | solution.py:374
  (3 shorter events, 0.0 us)
Async XLA Ops:
  2.5 7.6 %collective-permute-start = (f32[1,64,128]{2,1,0:T(8,128)S(1)}, f32[1,64,128]{2,1,0:T(8,128)S(1)}, u32[]{:S(2)}, u32[]{:S(2)}) collective-permute-start(f32[1,64,128]{2,1,0:T(8,128)S(1)} %get-tuple-element.20.refs_0_), channel_id=1, source_target_pairs={{0,16},{1,17},{2,18},{3,19},{4,20},{5,21},{6,22},{7,23},{8,24},{9,... | collective-permute-start | bytes 98312 | tf_op jit(solution)/shard_map/ppermute | solution.py:429
  6.6 5.2 %collective-permute-start.4 = (f32[1,72,128]{2,1,0:T(8,128)S(1)}, f32[1,72,128]{2,1,0:T(8,128)S(1)}, u32[]{:S(2)}, u32[]{:S(2)}) collective-permute-start(f32[1,72,128]{2,1,0:T(8,128)S(1)} %get-tuple-element.21.refs_1_), channel_id=1, source_target_pairs={{0,12},{1,13},{2,14},{3,15},{4,8},{5,9},{6,10},{7,11},{8,4},{9,5},... | collective-permute-start | bytes 110600 | tf_op jit(solution)/shard_map/ppermute | solution.py:429
  9.2 4.0 %collective-permute-start.3 = (f32[1,72,128]{2,1,0:T(8,128)S(1)}, f32[1,72,128]{2,1,0:T(8,128)S(1)}, u32[]{:S(2)}, u32[]{:S(2)}) collective-permute-start(f32[1,72,128]{2,1,0:T(8,128)S(1)} %get-tuple-element.21.refs_1_), channel_id=1, source_target_pairs={{0,8},{1,9},{2,10},{3,11},{4,12},{5,13},{6,14},{7,15},{8,0},{9,1},... | collective-permute-start | bytes 110600 | tf_op jit(solution)/shard_map/ppermute | solution.py:429
  9.6 4.0 %collective-permute-start.2 = (f32[1,72,128]{2,1,0:T(8,128)S(1)}, f32[1,72,128]{2,1,0:T(8,128)S(1)}, u32[]{:S(2)}, u32[]{:S(2)}) collective-permute-start(f32[1,72,128]{2,1,0:T(8,128)S(1)} %get-tuple-element.21.refs_1_), channel_id=1, source_target_pairs={{0,4},{1,5},{2,6},{3,7},{4,0},{5,1},{6,2},{7,3},{8,12},{9,13},{10,... | collective-permute-start | bytes 110600 | tf_op jit(solution)/shard_map/ppermute | solution.py:429
  10.1 5.3 %collective-permute-start.1 = (f32[2,64,128]{2,1,0:T(8,128)S(1)}, f32[2,64,128]{2,1,0:T(8,128)S(1)}, u32[]{:S(2)}, u32[]{:S(2)}) collective-permute-start(f32[2,64,128]{2,1,0:T(8,128)S(1)} %shard_map.51.refs_0_), channel_id=1, source_target_pairs={{0,2},{1,3},{2,0},{3,1},{4,6},{5,7},{6,4},{7,5},{8,10},{9,11},{10,... | collective-permute-start | bytes 196616 | tf_op jit(solution)/shard_map/ppermute | solution.py:429
  11.7 2.7 %collective-permute-start.5 = (f32[1,72,128]{2,1,0:T(8,128)S(1)}, f32[1,72,128]{2,1,0:T(8,128)S(1)}, u32[]{:S(2)}, u32[]{:S(2)}) collective-permute-start(f32[1,72,128]{2,1,0:T(8,128)S(1)} %get-tuple-element.21.refs_1_), channel_id=1, source_target_pairs={{0,1},{1,0},{2,3},{3,2},{4,5},{5,4},{6,7},{7,6},{8,9},{9,8},{10,11... | collective-permute-start | bytes 110600 | tf_op jit(solution)/shard_map/ppermute | solution.py:429
  11.9 2.5 %collective-permute-start.8 = (f32[1,72,128]{2,1,0:T(8,128)S(1)}, f32[1,72,128]{2,1,0:T(8,128)S(1)}, u32[]{:S(2)}, u32[]{:S(2)}) collective-permute-start(f32[1,72,128]{2,1,0:T(8,128)S(1)} %collective-permute-done.4.refs_4_), channel_id=1, source_target_pairs={{0,1},{1,0},{2,3},{3,2},{4,5},{5,4},{6,7},{7,6},{8,9},{9,8},{10,11... | collective-permute-start | bytes 110600 | tf_op jit(solution)/shard_map/ppermute | solution.py:429
  13.1 1.3 %collective-permute-start.7 = (f32[1,72,128]{2,1,0:T(8,128)S(1)}, f32[1,72,128]{2,1,0:T(8,128)S(1)}, u32[]{:S(2)}, u32[]{:S(2)}) collective-permute-start(f32[1,72,128]{2,1,0:T(8,128)S(1)} %collective-permute-done.3.refs_3_), channel_id=1, source_target_pairs={{0,1},{1,0},{2,3},{3,2},{4,5},{5,4},{6,7},{7,6},{8,9},{9,8},{10,11... | collective-permute-start | bytes 110600 | tf_op jit(solution)/shard_map/ppermute | solution.py:429
  13.6 1.2 %collective-permute-start.6 = (f32[1,72,128]{2,1,0:T(8,128)S(1)}, f32[1,72,128]{2,1,0:T(8,128)S(1)}, u32[]{:S(2)}, u32[]{:S(2)}) collective-permute-start(f32[1,72,128]{2,1,0:T(8,128)S(1)} %collective-permute-done.2.refs_2_), channel_id=1, source_target_pairs={{0,1},{1,0},{2,3},{3,2},{4,5},{5,4},{6,7},{7,6},{8,9},{9,8},{10,11... | collective-permute-start | bytes 110600 | tf_op jit(solution)/shard_map/ppermute | solution.py:429

commit v6 on v5

--- a/solution.py
+++ b/solution.py
@@ -170,21 +170,25 @@
 def project_kernel(features, projection_t, targets, latent, out, feature_buf, projection_buf, target_buf, sems):
     proj = projection_t.shape[0]
     chunks, height, _ = feature_buf.shape
-    copies = [
-        pltpu.make_async_copy(features.at[pl.ds(i * height, height)], feature_buf.at[i], sems.at[i])
-        for i in range(chunks)]
-    copies.insert(1, pltpu.make_async_copy(projection_t, projection_buf, sems.at[chunks]))
-    copies.append(pltpu.make_async_copy(targets, target_buf, sems.at[chunks + 1]))
-    for copy in copies:
+    some_rows = height // 2
+    streams = [[
+        pltpu.make_async_copy(
+            features.at[pl.ds(i * height + k * some_rows, some_rows)],
+            feature_buf.at[i, pl.ds(k * some_rows, some_rows)], sems.at[2 * i + k])
+        for k in range(2)] for i in range(chunks)]
+    matrix = pltpu.make_async_copy(projection_t, projection_buf, sems.at[2 * chunks])
+    last = pltpu.make_async_copy(targets, target_buf, sems.at[2 * chunks + 1])
+    for copy in (*streams[0], matrix, *[c for stream in streams[1:] for c in stream], last):
         copy.start()
-    copies.pop(1).wait()
+    matrix.wait()
     for i in range(chunks):
-        copies[i].wait()
+        for copy in streams[i]:
+            copy.wait()
         some = lax.dot_general(
             projection_buf[...], feature_buf[i], (((1,), (1,)), ((), ())), preferred_element_type=f32)
         latent[0, i * proj:(i + 1) * proj, :] = some
         out[0, i * proj:(i + 1) * proj, :] = some
-    copies[-1].wait()
+    last.wait()
     line = lax.broadcasted_iota(jnp.int32, (8, LANES), 0)
     tail = jnp.zeros((8, LANES), f32)
     for i in range(chunks):
@@ -457,7 +461,7 @@
         project_kernel, (shape(1, halves * proj, LANES), shape(1, halves * proj + 8, LANES)), *inputs,
         in_specs=[pl.BlockSpec(memory_space=pltpu.HBM)] * 3,
         scratch=[scratch(halves, LANES, feat, dtype=bf16), scratch(proj, feat, dtype=bf16),
-                 scratch(1, rows), pltpu.SemaphoreType.DMA((halves + 2,))])
+                 scratch(1, rows), pltpu.SemaphoreType.DMA((2 * halves + 2,))])
     row_parts, sides, flips = first_round(latent, own, wide, narrow)
     parts = len(row_parts)
     groups = narrow // parts

time: 40.1 us -> 40.2 us (level)
  no operation moved by 1% of the time
where the time goes in v6:
time: 40.2 us; the launch traced here: 40 us
  blocking collectives  21.5 us (53%)
  starting transfers between devices  9.55 us (24%)
  Pallas kernels  6.25 us (16%)
  waiting for transfers between devices  1.96 us (5%)
  between operations  0.68 us (2%)
    all_to_all x2, blocking collectives, to_all(): lax.all_to_all(blocks, ALL, split_axis=0, concat_axis=0, axis_index_group...  21.5 us
    ppermute x9, starting transfers between devices, swap(): return lax.ppermute(value, ALL, pairs)  9.55 us
    pallas_call x7, Pallas kernels, call(): pl.pallas_call(kernel, out_shape=out_shape, scratch_shapes=list(scratch),...  6.25 us
    ppermute x9, waiting for transfers between devices, swap(): return lax.ppermute(value, ALL, pairs)  1.96 us
  transfers between devices with their start and end apart: 9, of which 4 were waited for; matrix products, arithmetic and copies ran while one was open for 0% of the time, Pallas kernels for 3%

profile of v6, /device:TPU:0, one launch (start us, length us, event | category | flops | bytes accessed | tf_op | source)
XLA Modules:
  0.0 40.0 jit_solution(550675850688728397)
XLA Ops:
  0.6 1.9 %shard_map.50 = (f32[1,64,128]{2,1,0:T(8,128)S(1)}, f32[1,72,128]{2,1,0:T(8,128)S(1)}) custom-call(bf16[256,2048]{1,0:T(8,128)(2,1)} %features.1, bf16[32,2048]{1,0:T(8,128)(2,1)} %bitcast.4, f32[1,256]{1,0:T(1,128)} %bitcast.5), custom_call_target="tpu_custom_call" | custom-call | tf_op jit(solution)/shard_map/pallas_call | solution.py:378
  2.5 4.1 %collective-permute-start = (f32[1,64,128]{2,1,0:T(8,128)S(1)}, f32[1,64,128]{2,1,0:T(8,128)S(1)}, u32[]{:S(2)}, u32[]{:S(2)}) collective-permute-start(f32[1,64,128]{2,1,0:T(8,128)S(1)} %get-tuple-element.20.refs_0_), channel_id=1, source_target_pairs={{0,16},{1,17},{2,18},{3,19},{4,20},{5,21},{6,22},{7,23},{8,24},{9,... | collective-permute-start | bytes 98312 | tf_op jit(solution)/shard_map/ppermute | solution.py:433
  6.6 2.5 %collective-permute-start.4 = (f32[1,72,128]{2,1,0:T(8,128)S(1)}, f32[1,72,128]{2,1,0:T(8,128)S(1)}, u32[]{:S(2)}, u32[]{:S(2)}) collective-permute-start(f32[1,72,128]{2,1,0:T(8,128)S(1)} %get-tuple-element.21.refs_1_), channel_id=1, source_target_pairs={{0,12},{1,13},{2,14},{3,15},{4,8},{5,9},{6,10},{7,11},{8,4},{9,5},... | collective-permute-start | bytes 110600 | tf_op jit(solution)/shard_map/ppermute | solution.py:433
  9.2 0.4 %collective-permute-start.3 = (f32[1,72,128]{2,1,0:T(8,128)S(1)}, f32[1,72,128]{2,1,0:T(8,128)S(1)}, u32[]{:S(2)}, u32[]{:S(2)}) collective-permute-start(f32[1,72,128]{2,1,0:T(8,128)S(1)} %get-tuple-element.21.refs_1_), channel_id=1, source_target_pairs={{0,8},{1,9},{2,10},{3,11},{4,12},{5,13},{6,14},{7,15},{8,0},{9,1},... | collective-permute-start | bytes 110600 | tf_op jit(solution)/shard_map/ppermute | solution.py:433
  9.6 0.5 %collective-permute-start.2 = (f32[1,72,128]{2,1,0:T(8,128)S(1)}, f32[1,72,128]{2,1,0:T(8,128)S(1)}, u32[]{:S(2)}, u32[]{:S(2)}) collective-permute-start(f32[1,72,128]{2,1,0:T(8,128)S(1)} %get-tuple-element.21.refs_1_), channel_id=1, source_target_pairs={{0,4},{1,5},{2,6},{3,7},{4,0},{5,1},{6,2},{7,3},{8,12},{9,13},{10,... | collective-permute-start | bytes 110600 | tf_op jit(solution)/shard_map/ppermute | solution.py:433
  10.1 0.0 collective-permute-done.refs_1_
  10.1 1.6 %collective-permute-start.1 = (f32[2,64,128]{2,1,0:T(8,128)S(1)}, f32[2,64,128]{2,1,0:T(8,128)S(1)}, u32[]{:S(2)}, u32[]{:S(2)}) collective-permute-start(f32[2,64,128]{2,1,0:T(8,128)S(1)} %shard_map.51.refs_0_), channel_id=1, source_target_pairs={{0,2},{1,3},{2,0},{3,1},{4,6},{5,7},{6,4},{7,5},{8,10},{9,11},{10,... | collective-permute-start | bytes 196616 | tf_op jit(solution)/shard_map/ppermute | solution.py:433
  11.7 0.0 collective-permute-start.5
  11.7 0.2 collective-permute-done.4.refs_4_
  11.9 0.3 collective-permute-start.8
  12.2 0.9 %collective-permute-done.3.refs_3_ = f32[1,72,128]{2,1,0:T(8,128)S(1)} collective-permute-done((f32[1,72,128]{2,1,0:T(8,128)S(1)}, f32[1,72,128]{2,1,0:T(8,128)S(1)}, u32[]{:S(2)}, u32[]{:S(2)}) %collective-permute-start.3) | collective-permute-done | bytes 36896 | tf_op jit(solution)/shard_map/ppermute | solution.py:433
  13.1 0.4 %collective-permute-done.2.refs_2_ = f32[1,72,128]{2,1,0:T(8,128)S(1)} collective-permute-done((f32[1,72,128]{2,1,0:T(8,128)S(1)}, f32[1,72,128]{2,1,0:T(8,128)S(1)}, u32[]{:S(2)}, u32[]{:S(2)}) %collective-permute-start.2) | collective-permute-done | bytes 36896 | tf_op jit(solution)/shard_map/ppermute | solution.py:433
  13.6 0.1 collective-permute-start.6
  13.7 0.7 %shard_map.52 = (bf16[2,256,208]{2,1,0:T(8,128)(2,1)S(1)}, bf16[4,208,256]{2,1,0:T(8,128)(2,1)S(1)}, f32[8,128]{1,0:T(8,128)S(1)}, f32[4,128]{1,0:T(4,128)S(1)}, f32[2,4,256,256]{3,2,1,0:T(8,128)S(1)}) custom-call(f32[2,64,128]{2,1,0:T(8,128)S(1)} %shard_map.51.refs_0_, f32[1,72,128]{2,1,0:T(8,128)S(1)} %get-tuple-element.21.refs_1_, ...), custom_call_target="tpu_custom_call" | custom-call | flops 218103808 | bytes 2097152 | tf_op jit(solution)/shard_map/pallas_call | solution.py:378
  14.4 0.0 collective-permute-done.5.refs_1_
  14.4 0.0 collective-permute-done.8.refs_4_
  14.4 0.0 collective-permute-done.7.refs_3_
  14.4 0.4 collective-permute-done.6.refs_2_
  14.8 0.6 %shard_map.53 = (bf16[4,208,256]{2,1,0:T(8,128)(2,1)S(1)}, f32[8,128]{1,0:T(8,128)S(1)}, f32[4,128]{1,0:T(4,128)S(1)}, f32[2,4,256,256]{3,2,1,0:T(8,128)S(1)}) custom-call(bf16[2,256,208]{2,1,0:T(8,128)(2,1)S(1)} %get-tuple-element.24.refs_0_, f32[1,72,128]{2,1,0:T(8,128)S(1)} %collective-permute-done.5.refs_1_, ...), custom_call_target="tpu_custom_call" | custom-call | flops 218103808 | bytes 2097152 | tf_op jit(solution)/shard_map/pallas_call | solution.py:378
  15.5 1.1 %shard_map.54 = (f32[32,1,1280]{2,1,0:T(1,128)S(1)}, f32[2,4,256,256]{3,2,1,0:T(8,128)S(1)}, f32[2,4,256,256]{3,2,1,0:T(8,128)S(1)}) custom-call(f32[2,64,128]{2,1,0:T(8,128)S(1)} %collective-permute-done.1.refs_0_, bf16[4,208,256]{2,1,0:T(8,128)(2,1)S(1)} %get-tuple-element.22.refs_1_, f32[8,128]{1,0:T(8,128)S(1)} %get-tuple-element.23.refs_2_, ...), custom_call_target="tpu_custom_call" | custom-call | flops 436207616 | bytes 4194304 | tf_op jit(solution)/shard_map/pallas_call | solution.py:378
  16.5 11.7 %all_to_all.10.refs_0_ = f32[32,1,1280]{2,1,0:T(1,128)S(1)} all-to-all(f32[32,1,1280]{2,1,0:T(1,128)S(1)} %get-tuple-element.29), channel_id=1, replica_groups={{31,30,29,28,27,26,25,24,23,22,21,20,19,18,17,16,15,14,13,12,11,10,9,8,..., dimensions={0} | all-to-all | bytes 327680 | tf_op jit(solution)/shard_map/all_to_all | solution.py:389
  28.3 1.1 %shard_map.55 = (f32[32,1,384]{2,1,0:T(1,128)S(1)}, f32[5,128]{1,0:T(8,128)S(1)}) custom-call(f32[32,1,1280]{2,1,0:T(1,128)S(1)} %all_to_all.10.refs_0_, f32[2,4,256,256]{3,2,1,0:T(8,128)S(1)} %get-tuple-element.30.refs_1_, f32[2,4,256,256]{3,2,1,0:T(8,128)S(1)} %get-tuple-element.31.refs_2_, f32[2,4,256,256]{3,2,1,0:T(8,128)S(1)} %get-tuple-element.32.refs_3_, ...), custom_call_target="tpu_custom_call" | custom-call | tf_op jit(solution)/shard_map/pallas_call | solution.py:378
  29.3 9.8 %all_to_all.11.arrived = f32[32,1,384]{2,1,0:T(1,128)S(1)} all-to-all(f32[32,1,384]{2,1,0:T(1,128)S(1)} %get-tuple-element.34), channel_id=1, replica_groups={{31,30,29,28,27,26,25,24,23,22,21,20,19,18,17,16,15,14,13,12,11,10,9,8,..., dimensions={0} | all-to-all | bytes 98304 | tf_op jit(solution)/shard_map/all_to_all | solution.py:389
  39.1 0.8 %shard_map.56 = (f32[2,128]{1,0:T(2,128)}, f32[2,128]{1,0:T(2,128)}) custom-call(f32[32,1,384]{2,1,0:T(1,128)S(1)} %all_to_all.11.arrived, f32[5,128]{1,0:T(8,128)S(1)} %get-tuple-element.35.step_scalars), custom_call_target="tpu_custom_call" | custom-call | tf_op jit(solution)/shard_map/pallas_call | solution.py:378
  (3 shorter events, 0.0 us)
Async XLA Ops:
  2.5 7.6 %collective-permute-start = (f32[1,64,128]{2,1,0:T(8,128)S(1)}, f32[1,64,128]{2,1,0:T(8,128)S(1)}, u32[]{:S(2)}, u32[]{:S(2)}) collective-permute-start(f32[1,64,128]{2,1,0:T(8,128)S(1)} %get-tuple-element.20.refs_0_), channel_id=1, source_target_pairs={{0,16},{1,17},{2,18},{3,19},{4,20},{5,21},{6,22},{7,23},{8,24},{9,... | collective-permute-start | bytes 98312 | tf_op jit(solution)/shard_map/ppermute | solution.py:433
  6.6 5.2 %collective-permute-start.4 = (f32[1,72,128]{2,1,0:T(8,128)S(1)}, f32[1,72,128]{2,1,0:T(8,128)S(1)}, u32[]{:S(2)}, u32[]{:S(2)}) collective-permute-start(f32[1,72,128]{2,1,0:T(8,128)S(1)} %get-tuple-element.21.refs_1_), channel_id=1, source_target_pairs={{0,12},{1,13},{2,14},{3,15},{4,8},{5,9},{6,10},{7,11},{8,4},{9,5},... | collective-permute-start | bytes 110600 | tf_op jit(solution)/shard_map/ppermute | solution.py:433
  9.2 4.0 %collective-permute-start.3 = (f32[1,72,128]{2,1,0:T(8,128)S(1)}, f32[1,72,128]{2,1,0:T(8,128)S(1)}, u32[]{:S(2)}, u32[]{:S(2)}) collective-permute-start(f32[1,72,128]{2,1,0:T(8,128)S(1)} %get-tuple-element.21.refs_1_), channel_id=1, source_target_pairs={{0,8},{1,9},{2,10},{3,11},{4,12},{5,13},{6,14},{7,15},{8,0},{9,1},... | collective-permute-start | bytes 110600 | tf_op jit(solution)/shard_map/ppermute | solution.py:433
  9.6 4.0 %collective-permute-start.2 = (f32[1,72,128]{2,1,0:T(8,128)S(1)}, f32[1,72,128]{2,1,0:T(8,128)S(1)}, u32[]{:S(2)}, u32[]{:S(2)}) collective-permute-start(f32[1,72,128]{2,1,0:T(8,128)S(1)} %get-tuple-element.21.refs_1_), channel_id=1, source_target_pairs={{0,4},{1,5},{2,6},{3,7},{4,0},{5,1},{6,2},{7,3},{8,12},{9,13},{10,... | collective-permute-start | bytes 110600 | tf_op jit(solution)/shard_map/ppermute | solution.py:433
  10.1 5.3 %collective-permute-start.1 = (f32[2,64,128]{2,1,0:T(8,128)S(1)}, f32[2,64,128]{2,1,0:T(8,128)S(1)}, u32[]{:S(2)}, u32[]{:S(2)}) collective-permute-start(f32[2,64,128]{2,1,0:T(8,128)S(1)} %shard_map.51.refs_0_), channel_id=1, source_target_pairs={{0,2},{1,3},{2,0},{3,1},{4,6},{5,7},{6,4},{7,5},{8,10},{9,11},{10,... | collective-permute-start | bytes 196616 | tf_op jit(solution)/shard_map/ppermute | solution.py:433
  11.7 2.7 %collective-permute-start.5 = (f32[1,72,128]{2,1,0:T(8,128)S(1)}, f32[1,72,128]{2,1,0:T(8,128)S(1)}, u32[]{:S(2)}, u32[]{:S(2)}) collective-permute-start(f32[1,72,128]{2,1,0:T(8,128)S(1)} %get-tuple-element.21.refs_1_), channel_id=1, source_target_pairs={{0,1},{1,0},{2,3},{3,2},{4,5},{5,4},{6,7},{7,6},{8,9},{9,8},{10,11... | collective-permute-start | bytes 110600 | tf_op jit(solution)/shard_map/ppermute | solution.py:433
  11.9 2.5 %collective-permute-start.8 = (f32[1,72,128]{2,1,0:T(8,128)S(1)}, f32[1,72,128]{2,1,0:T(8,128)S(1)}, u32[]{:S(2)}, u32[]{:S(2)}) collective-permute-start(f32[1,72,128]{2,1,0:T(8,128)S(1)} %collective-permute-done.4.refs_4_), channel_id=1, source_target_pairs={{0,1},{1,0},{2,3},{3,2},{4,5},{5,4},{6,7},{7,6},{8,9},{9,8},{10,11... | collective-permute-start | bytes 110600 | tf_op jit(solution)/shard_map/ppermute | solution.py:433
  13.1 1.3 %collective-permute-start.7 = (f32[1,72,128]{2,1,0:T(8,128)S(1)}, f32[1,72,128]{2,1,0:T(8,128)S(1)}, u32[]{:S(2)}, u32[]{:S(2)}) collective-permute-start(f32[1,72,128]{2,1,0:T(8,128)S(1)} %collective-permute-done.3.refs_3_), channel_id=1, source_target_pairs={{0,1},{1,0},{2,3},{3,2},{4,5},{5,4},{6,7},{7,6},{8,9},{9,8},{10,11... | collective-permute-start | bytes 110600 | tf_op jit(solution)/shard_map/ppermute | solution.py:433
  13.6 1.2 %collective-permute-start.6 = (f32[1,72,128]{2,1,0:T(8,128)S(1)}, f32[1,72,128]{2,1,0:T(8,128)S(1)}, u32[]{:S(2)}, u32[]{:S(2)}) collective-permute-start(f32[1,72,128]{2,1,0:T(8,128)S(1)} %collective-permute-done.2.refs_2_), channel_id=1, source_target_pairs={{0,1},{1,0},{2,3},{3,2},{4,5},{5,4},{6,7},{7,6},{8,9},{9,8},{10,11... | collective-permute-start | bytes 110600 | tf_op jit(solution)/shard_map/ppermute | solution.py:433
